TPU v7x, 32 devices: a whole 2x2x4 slice. The times are simulated.
32 devices in a mesh: dp: 16 (over z, y, core), seq: 2 (over x).
Axes of the slice: x: 2, y: 2, z: 4, core: 2. Of those that a mesh axis runs over, the one named last changes fastest.
Arguments:
- tokens: bfloat16 [64, 1024, 1024], P('dp', 'seq'), may hold values from -6 to 6
- condition: float32 [64, 1024], P('dp'), may hold values from -6 to 6
- w_ada: bfloat16 [1024, 6144], P('dp', 'seq'), may hold values from -0.1875 to 0.1875
- b_ada: bfloat16 [6144], P(('dp', 'seq')), may hold values from -3 to 3
- w_qkv: bfloat16 [1024, 3072], P('dp', 'seq'), may hold values from -0.1875 to 0.1875
- q_bias: bfloat16 [1024], P(('dp', 'seq')), may hold values from -3 to 3
- v_bias: bfloat16 [1024], P(('dp', 'seq')), may hold values from -3 to 3
- w_proj: bfloat16 [1024, 1024], P('dp', 'seq'), may hold values from -0.5 to 0.5
- b_proj: bfloat16 [1024], P(('dp', 'seq')), may hold values from -3 to 3
- w_fc1: bfloat16 [1024, 4096], P('dp', 'seq'), may hold values from -0.1875 to 0.1875
- b_fc1: bfloat16 [4096], P(('dp', 'seq')), may hold values from -3 to 3
- w_fc2: bfloat16 [4096, 1024], P('dp', 'seq'), may hold values from -0.09375 to 0.09375
- b_fc2: bfloat16 [1024], P(('dp', 'seq')), may hold values from -3 to 3
- cotangent: bfloat16 [64, 1024, 1024], P('dp', 'seq'), may hold values from -6 to 6
Outputs:
- output: bfloat16 [64, 1024, 1024], P('dp', 'seq')
- grad_tokens: float32 [64, 1024, 1024], P('dp', 'seq')
- grad_condition: float32 [64, 1024], P('dp')
- grad_w_ada: float32 [1024, 6144], P('dp', 'seq')
- grad_b_ada: float32 [6144], P(('dp', 'seq'))
- grad_w_qkv: float32 [1024, 3072], P('dp', 'seq')
- grad_q_bias: float32 [1024], P(('dp', 'seq'))
- grad_v_bias: float32 [1024], P(('dp', 'seq'))
- grad_w_proj: float32 [1024, 1024], P('dp', 'seq')
- grad_b_proj: float32 [1024], P(('dp', 'seq'))
- grad_w_fc1: float32 [1024, 4096], P('dp', 'seq')
- grad_b_fc1: float32 [4096], P(('dp', 'seq'))
- grad_w_fc2: float32 [4096, 1024], P('dp', 'seq')
- grad_b_fc2: float32 [1024], P(('dp', 'seq'))
All inputs are finite; a program needn't handle non-finite values.
Results may differ from a plain program's by a relative error of at most 0.02.
Values may be sent and summed in bfloat16 or wider, within the bound.
No kernel may reach another device: no remote copies, remote signals or barrier semaphores. Data moves between devices by JAX's collectives and lax.ppermute only.
A program may use at most 704 MiB of HBM per device.

v0:
```python
import jax
import jax.numpy as jnp
from jax import lax
from jax.sharding import PartitionSpec as P

HEADS = 16


def normalize(rows):
    centre = rows - jnp.mean(rows, axis=-1, keepdims=True)
    return centre * lax.rsqrt(jnp.mean(centre * centre, axis=-1, keepdims=True) + 1e-06)


def gelu_tanh(value):
    return jax.nn.gelu(value, approximate=True)


def matmul(left, right):
    return jnp.dot(left, right, preferred_element_type=jnp.float32)


def contract_rows(left, right):
    return lax.dot_general(
        left, right, (((0,), (0,)), ((), ())), preferred_element_type=jnp.float32
    )


def contract_cols(left, right):
    return lax.dot_general(
        left, right, (((1,), (1,)), ((), ())), preferred_element_type=jnp.float32
    )


def collect_fore(w_ada, w_qkv, w_proj, w_fc1, w_fc2, b_ada, q_bias, v_bias, b_proj, b_fc1, b_fc2):
    inner = (
        lax.all_gather(w_ada, "seq", axis=1, tiled=True),
        lax.all_gather(w_qkv, "seq", axis=1, tiled=True),
        lax.all_gather(w_proj, "seq", axis=1, tiled=True),
        lax.all_gather(w_fc1, "seq", axis=1, tiled=True),
        lax.all_gather(w_fc2, "seq", axis=1, tiled=True),
        lax.all_gather(b_ada, "seq", axis=0, tiled=True),
        lax.all_gather(q_bias, "seq", axis=0, tiled=True),
        lax.all_gather(v_bias, "seq", axis=0, tiled=True),
        lax.all_gather(b_proj, "seq", axis=0, tiled=True),
        lax.all_gather(b_fc1, "seq", axis=0, tiled=True),
        lax.all_gather(b_fc2, "seq", axis=0, tiled=True),
    )
    return (
        lax.all_gather(inner[0], "dp", axis=0, tiled=True),
        lax.all_gather(inner[1], "dp", axis=0, tiled=True),
        lax.all_gather(inner[2], "dp", axis=0, tiled=True),
        lax.all_gather(inner[3], "dp", axis=0, tiled=True),
        lax.all_gather(inner[4], "dp", axis=0, tiled=True),
        lax.all_gather(inner[5], "dp", axis=0, tiled=True),
        lax.all_gather(inner[6], "dp", axis=0, tiled=True),
        lax.all_gather(inner[7], "dp", axis=0, tiled=True),
        lax.all_gather(inner[8], "dp", axis=0, tiled=True),
        lax.all_gather(inner[9], "dp", axis=0, tiled=True),
        lax.all_gather(inner[10], "dp", axis=0, tiled=True),
    )


def collect_back(w_ada, w_qkv, w_proj, w_fc1, w_fc2):
    inner = (
        lax.all_gather(w_ada, "seq", axis=1, tiled=True),
        lax.all_gather(w_qkv, "seq", axis=1, tiled=True),
        lax.all_gather(w_proj, "seq", axis=1, tiled=True),
        lax.all_gather(w_fc1, "seq", axis=1, tiled=True),
        lax.all_gather(w_fc2, "seq", axis=1, tiled=True),
    )
    return (
        lax.all_gather(inner[0], "dp", axis=0, tiled=True),
        lax.all_gather(inner[1], "dp", axis=0, tiled=True),
        lax.all_gather(inner[2], "dp", axis=0, tiled=True),
        lax.all_gather(inner[3], "dp", axis=0, tiled=True),
        lax.all_gather(inner[4], "dp", axis=0, tiled=True),
    )


def body(
    tokens,
    condition,
    w_ada,
    b_ada,
    w_qkv,
    q_bias,
    v_bias,
    w_proj,
    b_proj,
    w_fc1,
    b_fc1,
    w_fc2,
    b_fc2,
    cotangent,
):
    latents_here, tokens_here, model_width = tokens.shape
    head_count = HEADS
    head_size = model_width // head_count
    score_scale = head_size ** (-0.5)
    row_count = latents_here * tokens_here
    gathered = collect_fore(
        w_ada, w_qkv, w_proj, w_fc1, w_fc2, b_ada, q_bias, v_bias, b_proj, b_fc1, b_fc2
    )
    full_ada, full_qkv, full_proj, full_fc1, full_fc2 = (
        gathered[0],
        gathered[1],
        gathered[2],
        gathered[3],
        gathered[4],
    )
    bias_ada = gathered[5].astype(jnp.float32)
    bias_query = gathered[6].astype(jnp.float32)
    bias_value = gathered[7].astype(jnp.float32)
    bias_proj = gathered[8].astype(jnp.float32)
    bias_fc1 = gathered[9].astype(jnp.float32)
    bias_fc2 = gathered[10].astype(jnp.float32)
    inputs = tokens.astype(jnp.float32)
    smooth, silu_pull = jax.vjp(jax.nn.silu, condition)
    smooth_low = smooth.astype(jnp.bfloat16)
    mods = matmul(smooth_low, full_ada) + bias_ada
    pieces = [mods[:, None, index * model_width : (index + 1) * model_width] for index in range(6)]
    shift_one, scale_one, gate_one, shift_two, scale_two, gate_two = pieces
    normed_one, norm_pull_one = jax.vjp(normalize, inputs)
    first_rows = (
        (normed_one * (1.0 + scale_one) + shift_one)
        .astype(jnp.bfloat16)
        .reshape(row_count, model_width)
    )
    bias_row = jnp.concatenate([bias_query, jnp.zeros_like(bias_query), bias_value])
    projected = matmul(first_rows, full_qkv) + bias_row
    query = (
        projected[:, :model_width]
        .astype(jnp.bfloat16)
        .reshape(latents_here, tokens_here, head_count, head_size)
    )
    key_local = (
        projected[:, model_width : 2 * model_width]
        .astype(jnp.bfloat16)
        .reshape(latents_here, tokens_here, model_width)
    )
    value_local = (
        projected[:, 2 * model_width :]
        .astype(jnp.bfloat16)
        .reshape(latents_here, tokens_here, model_width)
    )
    key_all, value_all = (
        lax.all_gather(key_local, "seq", axis=1, tiled=True),
        lax.all_gather(value_local, "seq", axis=1, tiled=True),
    )
    key_count = key_all.shape[1]
    key_heads = key_all.reshape(latents_here, key_count, head_count, head_size)
    value_heads = value_all.reshape(latents_here, key_count, head_count, head_size)
    scores = (
        jnp.einsum("bqhd,bkhd->bhqk", query, key_heads, preferred_element_type=jnp.float32)
        * score_scale
    )
    peak = jnp.max(scores, axis=-1, keepdims=True)
    log_total = jnp.log(jnp.sum(jnp.exp(scores - peak), axis=-1, keepdims=True)) + peak
    softmaxed = jnp.exp(scores - log_total)
    attended = jnp.einsum(
        "bhqk,bkhd->bqhd",
        softmaxed.astype(jnp.bfloat16),
        value_heads,
        preferred_element_type=jnp.float32,
    )
    attended = attended.astype(jnp.bfloat16).reshape(row_count, model_width)
    attention = (matmul(attended, full_proj) + bias_proj).reshape(
        latents_here, tokens_here, model_width
    )
    middle = inputs + gate_one * attention
    normed_two, norm_pull_two = jax.vjp(normalize, middle)
    second_rows = (
        (normed_two * (1.0 + scale_two) + shift_two)
        .astype(jnp.bfloat16)
        .reshape(row_count, model_width)
    )
    hidden = matmul(second_rows, full_fc1) + bias_fc1
    active, gelu_pull = jax.vjp(gelu_tanh, hidden)
    active_low = active.astype(jnp.bfloat16)
    branch = (matmul(active_low, full_fc2) + bias_fc2).reshape(
        latents_here, tokens_here, model_width
    )
    output = (middle + gate_two * branch).astype(jnp.bfloat16)
    regained = collect_back(w_ada, w_qkv, w_proj, w_fc1, w_fc2)
    full_ada, full_qkv, full_proj, full_fc1, full_fc2 = (
        regained[0],
        regained[1],
        regained[2],
        regained[3],
        regained[4],
    )
    grad_out = cotangent.astype(jnp.float32)
    gate_two_grad = jnp.sum(grad_out * branch, axis=1)
    branch_grad = (gate_two * grad_out).astype(jnp.bfloat16).reshape(row_count, model_width)
    fc2_bias_grad = jnp.sum(branch_grad.astype(jnp.float32), axis=0)
    fc2_grad = contract_rows(active_low, branch_grad)
    active_grad = contract_cols(branch_grad, full_fc2)
    hidden_grad = gelu_pull(active_grad)[0].astype(jnp.bfloat16)
    fc1_bias_grad = jnp.sum(hidden_grad.astype(jnp.float32), axis=0)
    fc1_grad = contract_rows(second_rows, hidden_grad)
    second_grad = contract_cols(hidden_grad, full_fc1).reshape(
        latents_here, tokens_here, model_width
    )
    shift_two_grad = jnp.sum(second_grad, axis=1)
    scale_two_grad = jnp.sum(second_grad * normed_two, axis=1)
    middle_grad = grad_out + norm_pull_two(second_grad * (1.0 + scale_two))[0]
    gate_one_grad = jnp.sum(middle_grad * attention, axis=1)
    attention_grad = (gate_one * middle_grad).astype(jnp.bfloat16).reshape(row_count, model_width)
    proj_bias_grad = jnp.sum(attention_grad.astype(jnp.float32), axis=0)
    proj_grad = contract_rows(attended, attention_grad)
    attended_grad = contract_cols(attention_grad, full_proj).astype(jnp.bfloat16)
    attended_grad = attended_grad.reshape(latents_here, tokens_here, head_count, head_size)
    scores = (
        jnp.einsum("bqhd,bkhd->bhqk", query, key_heads, preferred_element_type=jnp.float32)
        * score_scale
    )
    softmaxed = jnp.exp(scores - log_total)
    weight_grad = jnp.einsum(
        "bqhd,bkhd->bhqk", attended_grad, value_heads, preferred_element_type=jnp.float32
    )
    row_delta = jnp.sum(softmaxed * weight_grad, axis=-1, keepdims=True)
    score_grad = (softmaxed * (weight_grad - row_delta)).astype(jnp.bfloat16)
    query_grad = (
        jnp.einsum("bhqk,bkhd->bqhd", score_grad, key_heads, preferred_element_type=jnp.float32)
        * score_scale
    )
    key_grad = (
        jnp.einsum("bhqk,bqhd->bkhd", score_grad, query, preferred_element_type=jnp.float32)
        * score_scale
    )
    value_grad = jnp.einsum(
        "bhqk,bqhd->bkhd",
        softmaxed.astype(jnp.bfloat16),
        attended_grad,
        preferred_element_type=jnp.float32,
    )
    key_mine, value_mine = (
        lax.psum_scatter(
            key_grad.reshape(latents_here, key_count, model_width).astype(jnp.bfloat16),
            "seq",
            scatter_dimension=1,
            tiled=True,
        ).astype(jnp.float32),
        lax.psum_scatter(
            value_grad.reshape(latents_here, key_count, model_width).astype(jnp.bfloat16),
            "seq",
            scatter_dimension=1,
            tiled=True,
        ).astype(jnp.float32),
    )
    query_low = query_grad.astype(jnp.bfloat16).reshape(row_count, model_width)
    value_low = value_mine.astype(jnp.bfloat16).reshape(row_count, model_width)
    joint_grad = jnp.concatenate(
        [query_low, key_mine.astype(jnp.bfloat16).reshape(row_count, model_width), value_low],
        axis=-1,
    )
    query_bias_grad = jnp.sum(query_low.astype(jnp.float32), axis=0)
    value_bias_grad = jnp.sum(value_low.astype(jnp.float32), axis=0)
    qkv_grad = contract_rows(first_rows, joint_grad)
    first_grad = contract_cols(joint_grad, full_qkv).reshape(latents_here, tokens_here, model_width)
    shift_one_grad = jnp.sum(first_grad, axis=1)
    scale_one_grad = jnp.sum(first_grad * normed_one, axis=1)
    input_grad = middle_grad + norm_pull_one(first_grad * (1.0 + scale_one))[0]
    mods_grad = jnp.concatenate(
        [
            shift_one_grad,
            scale_one_grad,
            gate_one_grad,
            shift_two_grad,
            scale_two_grad,
            gate_two_grad,
        ],
        axis=-1,
    )
    mods_low = lax.psum(mods_grad.astype(jnp.bfloat16), "seq")
    leader = (lax.axis_index("seq") == 0).astype(jnp.float32)
    ada_grad = contract_rows(smooth_low, mods_low) * leader
    ada_bias_grad = jnp.sum(mods_low.astype(jnp.float32), axis=0) * leader
    smooth_grad = contract_cols(mods_low, full_ada)
    condition_grad = silu_pull(smooth_grad)[0]
    summed = (
        lax.psum_scatter(
            ada_grad.astype(jnp.bfloat16), "dp", scatter_dimension=0, tiled=True
        ).astype(jnp.float32),
        lax.psum_scatter(
            qkv_grad.astype(jnp.bfloat16), "dp", scatter_dimension=0, tiled=True
        ).astype(jnp.float32),
        lax.psum_scatter(
            proj_grad.astype(jnp.bfloat16), "dp", scatter_dimension=0, tiled=True
        ).astype(jnp.float32),
        lax.psum_scatter(
            fc1_grad.astype(jnp.bfloat16), "dp", scatter_dimension=0, tiled=True
        ).astype(jnp.float32),
        lax.psum_scatter(
            fc2_grad.astype(jnp.bfloat16), "dp", scatter_dimension=0, tiled=True
        ).astype(jnp.float32),
        lax.psum_scatter(
            ada_bias_grad.astype(jnp.bfloat16), "dp", scatter_dimension=0, tiled=True
        ).astype(jnp.float32),
        lax.psum_scatter(
            query_bias_grad.astype(jnp.bfloat16), "dp", scatter_dimension=0, tiled=True
        ).astype(jnp.float32),
        lax.psum_scatter(
            value_bias_grad.astype(jnp.bfloat16), "dp", scatter_dimension=0, tiled=True
        ).astype(jnp.float32),
        lax.psum_scatter(
            proj_bias_grad.astype(jnp.bfloat16), "dp", scatter_dimension=0, tiled=True
        ).astype(jnp.float32),
        lax.psum_scatter(
            fc1_bias_grad.astype(jnp.bfloat16), "dp", scatter_dimension=0, tiled=True
        ).astype(jnp.float32),
        lax.psum_scatter(
            fc2_bias_grad.astype(jnp.bfloat16), "dp", scatter_dimension=0, tiled=True
        ).astype(jnp.float32),
    )
    owned = (
        lax.psum_scatter(
            summed[0].astype(jnp.bfloat16), "seq", scatter_dimension=1, tiled=True
        ).astype(jnp.float32),
        lax.psum_scatter(
            summed[1].astype(jnp.bfloat16), "seq", scatter_dimension=1, tiled=True
        ).astype(jnp.float32),
        lax.psum_scatter(
            summed[2].astype(jnp.bfloat16), "seq", scatter_dimension=1, tiled=True
        ).astype(jnp.float32),
        lax.psum_scatter(
            summed[3].astype(jnp.bfloat16), "seq", scatter_dimension=1, tiled=True
        ).astype(jnp.float32),
        lax.psum_scatter(
            summed[4].astype(jnp.bfloat16), "seq", scatter_dimension=1, tiled=True
        ).astype(jnp.float32),
        lax.psum_scatter(
            summed[5].astype(jnp.bfloat16), "seq", scatter_dimension=0, tiled=True
        ).astype(jnp.float32),
        lax.psum_scatter(
            summed[6].astype(jnp.bfloat16), "seq", scatter_dimension=0, tiled=True
        ).astype(jnp.float32),
        lax.psum_scatter(
            summed[7].astype(jnp.bfloat16), "seq", scatter_dimension=0, tiled=True
        ).astype(jnp.float32),
        lax.psum_scatter(
            summed[8].astype(jnp.bfloat16), "seq", scatter_dimension=0, tiled=True
        ).astype(jnp.float32),
        lax.psum_scatter(
            summed[9].astype(jnp.bfloat16), "seq", scatter_dimension=0, tiled=True
        ).astype(jnp.float32),
        lax.psum_scatter(
            summed[10].astype(jnp.bfloat16), "seq", scatter_dimension=0, tiled=True
        ).astype(jnp.float32),
    )
    return (
        output,
        input_grad,
        condition_grad,
        owned[0],
        owned[5],
        owned[1],
        owned[6],
        owned[7],
        owned[2],
        owned[8],
        owned[3],
        owned[9],
        owned[4],
        owned[10],
    )


def solution(mesh):
    return jax.shard_map(
        body,
        mesh=mesh,
        in_specs=(
            P("dp", "seq", None),
            P("dp", None),
            P("dp", "seq"),
            P(("dp", "seq")),
            P("dp", "seq"),
            P(("dp", "seq")),
            P(("dp", "seq")),
            P("dp", "seq"),
            P(("dp", "seq")),
            P("dp", "seq"),
            P(("dp", "seq")),
            P("dp", "seq"),
            P(("dp", "seq")),
            P("dp", "seq", None),
        ),
        out_specs=(
            P("dp", "seq", None),
            P("dp", "seq", None),
            P("dp", None),
            P("dp", "seq"),
            P(("dp", "seq")),
            P("dp", "seq"),
            P(("dp", "seq")),
            P(("dp", "seq")),
            P("dp", "seq"),
            P(("dp", "seq")),
            P("dp", "seq"),
            P(("dp", "seq")),
            P("dp", "seq"),
            P(("dp", "seq")),
        ),
        check_vma=False,
    )
```

profile of v0, /device:TPU:0, one launch (start us, length us, event | category | flops | bytes accessed | tf_op | source)
XLA Modules:
  0.0 1812.1 jit_solution(16269870922443054299)
XLA Ops:
  7.2 14.8 all_gather.82
  42.6 33.8 %all-reduce.22 = (bf16[1024]{0:T(1024)(128)(2,1)S(1)}, bf16[1024]{0:T(1024)(128)(2,1)S(1)}, bf16[1024]{0:T(1024)(128)(2,1)S(1)}, bf16[1024]{0:T(1024)(128)(2,1)S(1)}) all-reduce(bf16[1024]{0:T(1024)(128)(2,1)S(1)} %dynamic-update-slice.6, bf16[1024]{0:T(1024)(128)(2,1)S(1)} %dynamic-update-slice.4, ...), channel_id=1, replica_groups=mesh['dp'=16,'seq'=2] {'dp'}, use_global_device_ids=true, to_apply=%add.6 | all-reduce | flops 4096 | bytes 16384
  76.4 17.6 all-gather
  100.6 23.5 %all-gather.11.cloned.1.call-done = bf16[1024,6144]{1,0:T(8,128)(2,1)} async-done(((bf16[64,6144]{1,0:T(8,128)(2,1)}), bf16[1024,6144]{1,0:T(8,128)(2,1)}) %all-gather.11.cloned.1.call-update) | async-done | bytes 12582928 | tf_op jit(solution)/shard_map/all_gather | solution.py:49
  134.8 51.8 %all-gather.13.cloned.1.call-done = bf16[1024,3072]{1,0:T(8,128)(2,1)} async-done(((bf16[64,3072]{1,0:T(8,128)(2,1)}), bf16[1024,3072]{1,0:T(8,128)(2,1)}) %all-gather.13.cloned.1.call-update) | async-done | bytes 6291472 | tf_op jit(solution)/shard_map/all_gather | solution.py:50
  186.5 16.5 add_convert_fusion
  214.0 12.3 all_gather.98
  226.3 13.8 all_gather.102
  245.7 17.1 all-gather.2
  263.4 11.5 reshape.242
  275.0 9.8 copy.65
  290.9 26.8 %all-gather.17.cloned.1.call-done = bf16[4,1024,1024]{2,1,0:T(8,128)(2,1)} async-done(((bf16[4,512,1024]{2,1,0:T(8,128)(2,1)}), bf16[4,1024,1024]{2,1,0:T(8,128)(2,1)}) %all-gather.17.cloned.1.call-update) | async-done | bytes 8388624 | tf_op jit(solution)/shard_map/all_gather | solution.py:147
  317.7 11.8 copy.64
  329.5 50.4 %multiply_reduce_fusion.1 = (f32[4,16,512]{2,1,0:T(8,128)S(1)}, f32[4,16,512,1024]{3,2,1,0:T(8,128)}) fusion(bf16[4,512,16,64]{1,3,2,0:T(8,128)(2,1)} %copy.65, bf16[4,1024,16,64]{1,3,2,0:T(8,128)(2,1)} %bitcast.95), kind=kOutput, calls=%fused_computation.4 | convolution fusion | flops 4362043392 | bytes 146931712 | tf_op jit(solution)/shard_map/bqhd,bkhd->bhqk/dot_general | solution.py:154
  379.9 41.1 %exponential_reduce_fusion = f32[4,16,512]{2,1,0:T(8,128)S(1)} fusion(f32[4,16,512,1024]{3,2,1,0:T(8,128)} %get-tuple-element.66, f32[4,16,512]{2,1,0:T(8,128)S(1)} %get-tuple-element.65), kind=kLoop, calls=%fused_computation.3 | loop fusion | flops 100630528 | bytes 134479872 | tf_op jit(solution)/shard_map/reduce_sum | solution.py:158
  421.8 11.4 copy.62
  433.2 48.9 %convert_bitcast_fusion = bf16[4,512,16,64]{1,3,2,0:T(8,128)(2,1)} fusion(bf16[4,1024,16,64]{1,3,2,0:T(8,128)(2,1)} %bitcast.93, f32[4,16,512,1024]{3,2,1,0:T(8,128)} %get-tuple-element.66, f32[4,16,512]{2,1,0:T(8,128)S(1)} %log_add_fusion), kind=kOutput, calls=%fused_computation.64 | convolution fusion | flops 4397727744 | bytes 146931712 | tf_op jit(solution)/shard_map/bhqk,bkhd->bqhd/dot_general | solution.py:160
  491.1 11.4 broadcast_add_fusion
  513.3 27.6 %all-gather.21.cloned.1.call-done = bf16[1024,4096]{1,0:T(8,128)(2,1)} async-done(((bf16[64,4096]{1,0:T(8,128)(2,1)}), bf16[1024,4096]{1,0:T(8,128)(2,1)}) %all-gather.21.cloned.1.call-update) | async-done | bytes 8388624 | tf_op jit(solution)/shard_map/all_gather | solution.py:52
  540.9 35.6 %multiply_convert_fusion.1 = (bf16[2048,4096]{1,0:T(8,128)(2,1)}, f32[2048,4096]{1,0:T(8,128)}) fusion(f32[4096]{0:T(1024)S(1)} %bitcast.121, bf16[2048,1024]{1,0:T(8,128)(2,1)} %bitcast.113, bf16[1024,4096]{1,0:T(8,128)(2,1)} %all-gather.21.cloned.1.call-done), kind=kOutput, calls=%fused_computation.15 | convolution fusion | flops 17263755264 | bytes 62930944 | tf_op jit(solution)/shard_map/dot_general | solution.py:19
  576.5 39.8 %all-gather.23.cloned.1.call-done = bf16[4096,1024]{1,0:T(8,128)(2,1)} async-done(((bf16[256,1024]{1,0:T(8,128)(2,1)}), bf16[4096,1024]{1,0:T(8,128)(2,1)}) %all-gather.23.cloned.1.call-update) | async-done | bytes 8388624 | tf_op jit(solution)/shard_map/all_gather | solution.py:53
  616.3 47.9 %fusion.51 = (bf16[4096]{0:T(1024)(128)(2,1)}, bf16[2048,4096]{1,0:T(8,128)(2,1)}) fusion(f32[2048,4096]{1,0:T(8,128)} %get-tuple-element.68, f32[4096]{0:T(1024)S(1)} %bitcast.122, bf16[2048,1024]{1,0:T(8,128)(2,1)} %bitcast.109, bf16[4096,1024]{1,0:T(8,128)(2,1)} %all-gather.23.cloned.1.call-done), kind=kOutput, calls=%fused_computation.113 | convolution fusion | flops 17364414464 | bytes 62939136 | tf_op jit(solution)/shard_map/dot_general | solution.py:29
  664.1 24.7 %fusion.52 = f32[2048,1024]{1,0:T(8,128)} fusion(bf16[2048,4096]{1,0:T(8,128)(2,1)} %get-tuple-element.74, bf16[1024,4096]{1,0:T(8,128)(2,1)} %all-gather.21.cloned.1.call-done), kind=kOutput, calls=%fused_computation.114 | convolution fusion | flops 17179869184 | bytes 33554432 | tf_op jit(solution)/shard_map/dot_general | solution.py:29
  698.0 21.5 %convolution_add_fusion.1 = f32[2048,1024]{1,0:T(8,128)} fusion(bf16[2048,4096]{1,0:T(8,128)(2,1)} %get-tuple-element.67, bf16[4096,1024]{1,0:T(8,128)(2,1)S(1)} %copy-done.41, f32[1024]{0:T(1024)S(1)} %copy-done.39), kind=kOutput, calls=%fused_computation.61 | convolution fusion | flops 17181966336 | bytes 33558528 | tf_op jit(solution)/shard_map/dot_general | solution.py:19
  719.5 9.8 add_add_fusion.1
  747.8 11.6 reshape.243
  759.5 9.8 copy.68
  769.2 48.8 %fusion.26 = bf16[4,16,64,1024]{3,2,1,0:T(8,128)(2,1)} fusion(bf16[4,512,16,64]{1,3,2,0:T(8,128)(2,1)} %copy.68, f32[4,16,512,1024]{3,2,1,0:T(8,128)} %get-tuple-element.66, f32[4,16,512]{2,1,0:T(8,128)S(1)} %copy-done.8), kind=kOutput, calls=%fused_computation.57 | convolution fusion | flops 4399824896 | bytes 146931712 | tf_op jit(solution)/shard_map/bhqk,bqhd->bkhd/dot_general | solution.py:231
  818.0 11.4 copy.73
  829.4 98.5 %multiply_reduce_fusion = (f32[4,16,512]{2,1,0:T(8,128)S(1)}, f32[4,16,512,1024]{3,2,1,0:T(8,128)}) fusion(f32[4,16,512,1024]{3,2,1,0:T(8,128)} %get-tuple-element.66, f32[4,16,512]{2,1,0:T(8,128)S(1)} %copy-done.8, bf16[4,512,16,64]{1,3,2,0:T(8,128)(2,1)} %copy.68, bf16[4,1024,16,64]{1,3,2,0:T(8,128)(2,1)} %bitcast.94), kind=kOutput, calls=%fused_computation.1 | convolution fusion | flops 4429152256 | bytes 281280512 | tf_op jit(solution)/shard_map/bqhd,bkhd->bhqk/dot_general | solution.py:218
  927.9 103.3 %multiply_convert_fusion = bf16[4,16,512,1024]{3,2,1,0:T(8,128)(2,1)} fusion(f32[4,16,512,1024]{3,2,1,0:T(8,128)} %get-tuple-element.70, f32[4,16,512,1024]{3,2,1,0:T(8,128)} %get-tuple-element.66, f32[4,16,512]{2,1,0:T(8,128)S(1)} %get-tuple-element.69, f32[4,16,512]{2,1,0:T(8,128)S(1)} %copy-done.8), kind=kLoop, calls=%fused_computation | loop fusion | flops 167772160 | bytes 335806464 | tf_op jit(solution)/shard_map/convert_element_type | solution.py:222
  1031.2 28.0 %multiply_convert_fusion.3 = bf16[4,16,64,1024]{3,2,1,0:T(8,128)(2,1)} fusion(bf16[4,512,16,64]{1,3,2,0:T(8,128)(2,1)} %copy.65, bf16[4,16,512,1024]{3,2,1,0:T(8,128)(2,1)} %multiply_convert_fusion), kind=kOutput, calls=%fused_computation.18 | convolution fusion | flops 4303355904 | bytes 79691776 | tf_op jit(solution)/shard_map/bhqk,bqhd->bkhd/dot_general | solution.py:228
  1059.2 11.4 copy.71
  1070.7 9.3 convolution_convert_fusion.4
  1080.0 24.5 %convolution_convert_fusion = bf16[4096,1024]{1,0:T(8,128)(2,1)} fusion(bf16[2048,4096]{1,0:T(8,128)(2,1)} %get-tuple-element.67, bf16[2048,1024]{1,0:T(8,128)(2,1)} %bitcast.110), kind=kOutput, calls=%fused_computation.55 | convolution fusion | flops 17184063488 | bytes 29360128 | tf_op jit(solution)/shard_map/dot_general | solution.py:23
  1104.6 23.5 %convolution_convert_fusion.1 = bf16[1024,4096]{1,0:T(8,128)(2,1)} fusion(bf16[2048,1024]{1,0:T(8,128)(2,1)} %bitcast.114, bf16[2048,4096]{1,0:T(8,128)(2,1)} %get-tuple-element.74), kind=kOutput, calls=%fused_computation.56 | convolution fusion | flops 17184063488 | bytes 29360128 | tf_op jit(solution)/shard_map/dot_general | solution.py:23
  1128.2 33.7 %fusion.50 = (bf16[16,64]{1,0:T(8,128)(2,1)S(1)}, bf16[4,512,16,64]{1,3,2,0:T(8,128)(2,1)}) fusion(bf16[4,1024,16,64]{1,3,2,0:T(8,128)(2,1)} %bitcast.96, bf16[4,16,512,1024]{3,2,1,0:T(8,128)(2,1)} %multiply_convert_fusion), kind=kOutput, calls=%fused_computation.112 | convolution fusion | flops 4301257728 | bytes 79693824 | tf_op jit(solution)/shard_map/bhqk,bkhd->bqhd/dot_general | solution.py:224
  1184.0 19.6 %convolution_convert_fusion.2 = bf16[1024,3072]{1,0:T(8,128)(2,1)} fusion(bf16[2048,1024]{1,0:T(8,128)(2,1)} %bitcast.112, bf16[2048,1024]{0,1:T(8,128)(2,1)} %copy.75, bf16[2048,1024]{0,1:T(8,128)(2,1)} %copy.74, bf16[2048,1024]{0,1:T(8,128)(2,1)} %bitcast.117), kind=kOutput, calls=%fused_computation.59 | convolution fusion | flops 12925796352 | bytes 23068672 | tf_op jit(solution)/shard_map/dot_general | solution.py:23
  1203.7 29.7 %reduce-scatter.25.cloned.1.call-done = bf16[64,1024]{1,0:T(8,128)(2,1)} async-done(((bf16[1024,1024]{1,0:T(8,128)(2,1)}), bf16[64,1024]{1,0:T(8,128)(2,1)}) %reduce-scatter.25.cloned.1.call-update) | async-done | bytes 131088 | tf_op jit(solution)/shard_map/reduce_scatter | solution.py:288
  1233.5 108.2 %reduce-scatter.33.cloned.1.call-done = bf16[256,1024]{1,0:T(8,128)(2,1)} async-done(((bf16[4096,1024]{1,0:T(8,128)(2,1)}), bf16[256,1024]{1,0:T(8,128)(2,1)}) %reduce-scatter.33.cloned.1.call-update) | async-done | bytes 524304 | tf_op jit(solution)/shard_map/reduce_scatter | solution.py:294
  1341.8 109.4 %reduce-scatter.29.cloned.1.call-done = bf16[64,4096]{1,0:T(8,128)(2,1)} async-done(((bf16[1024,4096]{1,0:T(8,128)(2,1)}), bf16[64,4096]{1,0:T(8,128)(2,1)}) %reduce-scatter.29.cloned.1.call-update) | async-done | bytes 524304 | tf_op jit(solution)/shard_map/reduce_scatter | solution.py:291
  1451.2 20.3 %fusion.29 = f32[2048,1024]{1,0:T(8,128)} fusion(bf16[1024,3072]{1,0:T(8,128)(2,1)} %all-gather.13.cloned.1.call-done, bf16[2048,1024]{0,1:T(8,128)(2,1)} %copy.75, bf16[2048,1024]{0,1:T(8,128)(2,1)} %copy.74, bf16[2048,1024]{0,1:T(8,128)(2,1)} %bitcast.118), kind=kOutput, calls=%fused_computation.60 | convolution fusion | flops 12922650624 | bytes 27262976 | tf_op jit(solution)/shard_map/dot_general | solution.py:29
  1485.2 11.9 fusion.24
  1512.6 28.0 %reduce-scatter.21.cloned.1.call-done = bf16[64,3072]{1,0:T(8,128)(2,1)} async-done(((bf16[1024,3072]{1,0:T(8,128)(2,1)}), bf16[64,3072]{1,0:T(8,128)(2,1)}) %reduce-scatter.21.cloned.1.call-update) | async-done | bytes 393232 | tf_op jit(solution)/shard_map/reduce_scatter | solution.py:285
  1553.9 15.2 reduce-scatter.35.cloned.1.call-done
  1570.8 15.0 reduce-scatter.31.cloned.1.call-done
  1590.5 133.8 %reduce-scatter.17.cloned.1.call-done = bf16[64,6144]{1,0:T(8,128)(2,1)} async-done(((bf16[1024,6144]{1,0:T(8,128)(2,1)}), bf16[64,6144]{1,0:T(8,128)(2,1)}) %reduce-scatter.17.cloned.1.call-update) | async-done | bytes 786448 | tf_op jit(solution)/shard_map/reduce_scatter | solution.py:282
  1724.4 59.6 %all-reduce.21 = (bf16[6144]{0:T(1024)(128)(2,1)S(1)}, bf16[1024]{0:T(1024)(128)(2,1)S(1)}, bf16[1024]{0:T(1024)(128)(2,1)S(1)}, bf16[1024]{0:T(1024)(128)(2,1)S...) all-reduce(bf16[6144]{0:T(1024)(128)(2,1)S(1)} %multiply_convert_fu, ...), channel_id=6, replica_groups=mesh['dp'=16,'seq'=2] {'dp'}, use_global_device_ids=true, to_apply=%region_23.24.clone | all-reduce | flops 14336 | bytes 57344
  (232 shorter events, 196.0 us)
Async XLA Ops:
  7.2 116.9 %copy-start.17 = (f32[4,1024]{1,0:T(4,128)S(1)}, f32[4,1024]{1,0:T(4,128)}, u32[]{:S(2)}) copy-start(f32[4,1024]{1,0:T(4,128)} %param.15) | copy-start | bytes 49156
  7.2 116.8 %all-gather.11.cloned.1.call-start = ((), (), s32[]{:S(2)}) async-start(), calls=%async_computation.12 | async-start | bytes 13369344 | tf_op jit(solution)/shard_map/all_gather | solution.py:49
  22.0 164.5 %all-gather.13.cloned.1.call-start = ((), (), s32[]{:S(2)}) async-start(), calls=%async_computation.13 | async-start | bytes 6684672 | tf_op jit(solution)/shard_map/all_gather | solution.py:50
  29.2 288.5 %all-gather.17.cloned.1.call-start = ((), (), s32[]{:S(2)}) async-start(), calls=%async_computation.15 | async-start | bytes 12582912 | tf_op jit(solution)/shard_map/all_gather | solution.py:147
  96.9 34.2 %copy-start.12 = (f32[4,512]{1,0:T(4,128)}, f32[4,512]{1,0:T(4,128)S(1)}, u32[]{:S(2)}) copy-start(f32[4,512]{1,0:T(4,128)S(1)} %broadcast_multiply_fusion.1) | copy-start | bytes 24580
  100.6 30.6 %copy-start.23 = (f32[4,512]{1,0:T(4,128)}, f32[4,512]{1,0:T(4,128)S(1)}, u32[]{:S(2)}) copy-start(f32[4,512]{1,0:T(4,128)S(1)} %fusion.36) | copy-start | bytes 24580
  131.1 153.6 %copy-start.19 = (f32[4,1024]{1,0:T(4,128)}, f32[4,1024]{1,0:T(4,128)S(1)}, u32[]{:S(2)}) copy-start(f32[4,1024]{1,0:T(4,128)S(1)} %get-tuple-element.55) | copy-start | bytes 49156
  207.8 18.5 %copy-start.16 = (bf16[256,512]{1,0:T(8,128)(2,1)S(1)}, bf16[256,512]{1,0:T(8,128)(2,1)}, u32[]{:S(2)}) copy-start(bf16[256,512]{1,0:T(8,128)(2,1)} %param.25) | copy-start | bytes 786436
  207.8 32.4 %copy-start.43 = (bf16[128]{0:T(256)(128)(2,1)S(1)}, bf16[128]{0:T(256)(128)(2,1)}, u32[]{:S(2)}) copy-start(bf16[128]{0:T(256)(128)(2,1)} %param.24) | copy-start | bytes 772
  207.8 213.9 %all-gather.15.cloned.1.call-start = ((), (), s32[]{:S(2)}) async-start(), calls=%async_computation.14 | async-start | bytes 12582912 | tf_op jit(solution)/shard_map/all_gather | solution.py:148
  208.4 282.7 %all-gather.19.cloned.1.call-start = ((), (), s32[]{:S(2)}) async-start(), calls=%async_computation.16 | async-start | bytes 2228224 | tf_op jit(solution)/shard_map/all_gather | solution.py:51
  213.9 327.0 %all-gather.21.cloned.1.call-start = ((), (), s32[]{:S(2)}) async-start(), calls=%async_computation.17 | async-start | bytes 8912896 | tf_op jit(solution)/shard_map/all_gather | solution.py:52
  226.3 390.0 %all-gather.23.cloned.1.call-start = ((), (), s32[]{:S(2)}) async-start(), calls=%async_computation.18 | async-start | bytes 8912896 | tf_op jit(solution)/shard_map/all_gather | solution.py:53
  240.2 930.8 %reduce-scatter.15.cloned.1.call-start = ((), (), s32[]{:S(2)}) async-start(), calls=%async_computation.20 | async-start | bytes 12582912 | tf_op jit(solution)/shard_map/reduce_scatter | solution.py:244
  433.1 48.9 %copy-start.7 = (f32[4,16,512]{2,1,0:T(8,128)}, f32[4,16,512]{2,1,0:T(8,128)S(1)}, u32[]{:S(2)}) copy-start(f32[4,16,512]{2,1,0:T(8,128)S(1)} %log_add_fusion) | copy-start | bytes 393220
  482.0 9.1 copy-start.40
  491.1 11.4 copy-start.3
  491.1 11.4 copy-start.21
  509.4 31.5 %copy-start.35 = (f32[16,1,256]{2,1,0:T(1,128)S(1)}, f32[16,1,256]{2,1,0:T(1,128)}, u32[]{:S(2)}) copy-start(f32[16,1,256]{2,1,0:T(1,128)} %convert_element_type.234) | copy-start | bytes 49156
  664.1 24.7 %copy-start.1 = (f32[4,512,1024]{2,1,0:T(8,128)S(1)}, f32[4,512,1024]{2,1,0:T(8,128)}, u32[]{:S(2)}) copy-start(f32[4,512,1024]{2,1,0:T(8,128)} %copy-done) | copy-start | bytes 25165828
  688.8 9.2 copy-start.28
  688.8 9.2 copy-start.39
  688.8 9.2 copy-start.41
  698.0 21.5 %copy-start.20 = (f32[4,1024]{1,0:T(4,128)S(1)}, f32[4,1024]{1,0:T(4,128)}, u32[]{:S(2)}) copy-start(f32[4,1024]{1,0:T(4,128)} %copy-done.19) | copy-start | bytes 49156
  733.2 8.2 copy-start.42
  759.5 9.8 copy-start.8
  829.4 348.1 %reduce-scatter.13.cloned.1.call-start = ((), (), s32[]{:S(2)}) async-start(), calls=%async_computation.19 | async-start | bytes 12582912 | tf_op jit(solution)/shard_map/reduce_scatter | solution.py:238
  1070.6 162.8 %reduce-scatter.25.cloned.1.call-start = ((), (), s32[]{:S(2)}) async-start(), calls=%async_computation.25 | async-start | bytes 2228224 | tf_op jit(solution)/shard_map/reduce_scatter | solution.py:288
  1080.0 261.7 %reduce-scatter.33.cloned.1.call-start = ((), (), s32[]{:S(2)}) async-start(), calls=%async_computation.29 | async-start | bytes 8912896 | tf_op jit(solution)/shard_map/reduce_scatter | solution.py:294
  1104.5 346.6 %reduce-scatter.29.cloned.1.call-start = ((), (), s32[]{:S(2)}) async-start(), calls=%async_computation.27 | async-start | bytes 8912896 | tf_op jit(solution)/shard_map/reduce_scatter | solution.py:291
  1128.1 412.4 %reduce-scatter.21.cloned.1.call-start = ((), (), s32[]{:S(2)}) async-start(), calls=%async_computation.23 | async-start | bytes 6684672 | tf_op jit(solution)/shard_map/reduce_scatter | solution.py:285
  1203.7 348.7 %reduce-scatter.27.cloned.1.call-start = ((), (), s32[]{:S(2)}) async-start(), calls=%async_computation.26 | async-start | bytes 196608 | tf_op jit(solution)/shard_map/reduce_scatter | solution.py:323
  1233.4 335.6 %reduce-scatter.35.cloned.1.call-start = ((), (), s32[]{:S(2)}) async-start(), calls=%async_computation.30 | async-start | bytes 786432 | tf_op jit(solution)/shard_map/reduce_scatter | solution.py:329
  1341.7 244.1 %reduce-scatter.31.cloned.1.call-start = ((), (), s32[]{:S(2)}) async-start(), calls=%async_computation.28 | async-start | bytes 786432 | tf_op jit(solution)/shard_map/reduce_scatter | solution.py:326
  1451.1 20.4 %copy-start.11 = (f32[4,1024]{1,0:T(4,128)S(1)}, f32[4,1024]{1,0:T(4,128)}, u32[]{:S(2)}) copy-start(f32[4,1024]{1,0:T(4,128)} %copy-done.10) | copy-start | bytes 49156
  1451.1 20.4 %copy-start.13 = (f32[4,512]{1,0:T(4,128)S(1)}, f32[4,512]{1,0:T(4,128)}, u32[]{:S(2)}) copy-start(f32[4,512]{1,0:T(4,128)} %copy-done.12) | copy-start | bytes 24580
  1451.2 273.2 %reduce-scatter.17.cloned.1.call-start = ((), (), s32[]{:S(2)}) async-start(), calls=%async_computation.21 | async-start | bytes 13369344 | tf_op jit(solution)/shard_map/reduce_scatter | solution.py:282
  1471.5 9.2 copy-start.5
  1471.5 9.2 copy-start.24
  1471.6 13.5 slice-start
  1485.2 12.0 copy-start.34
  1485.2 12.0 copy-start.33
  1485.2 20.9 %copy-start.18 = (f32[4,1024]{1,0:T(4,128)S(1)}, f32[4,1024]{1,0:T(4,128)}, u32[]{:S(2)}) copy-start(f32[4,1024]{1,0:T(4,128)} %param.15) | copy-start | bytes 49156
  1512.5 211.9 %copy-start.36 = (bf16[1024]{0:T(1024)(128)(2,1)S(1)}, bf16[1024]{0:T(1024)(128)(2,1)}, u32[]{:S(2)}) copy-start(bf16[1024]{0:T(1024)(128)(2,1)} %get-tuple-element.43) | copy-start | bytes 6148
  1512.5 211.9 %copy-start.37 = (bf16[1024]{0:T(1024)(128)(2,1)S(1)}, bf16[1024]{0:T(1024)(128)(2,1)}, u32[]{:S(2)}) copy-start(bf16[1024]{0:T(1024)(128)(2,1)} %get-tuple-element.45) | copy-start | bytes 6148
  1512.5 211.9 %copy-start.38 = (bf16[4096]{0:T(1024)(128)(2,1)S(1)}, bf16[4096]{0:T(1024)(128)(2,1)}, u32[]{:S(2)}) copy-start(bf16[4096]{0:T(1024)(128)(2,1)} %get-tuple-element.73) | copy-start | bytes 24580
  1512.6 289.0 %reduce-scatter.23.cloned.1.call-start = ((), (), s32[]{:S(2)}) async-start(), calls=%async_computation.24 | async-start | bytes 589824 | tf_op jit(solution)/shard_map/reduce_scatter | solution.py:320
  1540.6 262.6 %reduce-scatter.19.cloned.1.call-start = ((), (), s32[]{:S(2)}) async-start(), calls=%async_computation.22 | async-start | bytes 1179648 | tf_op jit(solution)/shard_map/reduce_scatter | solution.py:317
  (17 other events, 65.1 us)
Sparse Core Ops, SparseCore 0:
  22.1 101.8 all-gather.10
  126.3 60.1 all-gather.12
  207.9 109.7 all-gather.16
  319.1 102.5 all-gather.14
  423.8 41.3 all-gather.18
  467.2 73.6 all-gather.20
  543.1 73.1 all-gather.22
  829.5 97.4 reduce-scatter.14
  1070.8 97.4 reduce-scatter.12
  1171.8 61.5 reduce-scatter.24
  1238.0 103.6 reduce-scatter.32
  1346.7 104.3 reduce-scatter.28
  1455.6 84.9 reduce-scatter.20
  1542.6 9.6 reduce-scatter.26
  1554.4 14.5 reduce-scatter.34
  1571.2 14.5 reduce-scatter.30
  1589.7 134.6 reduce-scatter.16
  1726.5 12.2 reduce-scatter.22
  1741.1 17.4 reduce-scatter.18
where the time goes:
time: 1820 us; the launch traced here: 1810 us
  waiting for transfers between devices  618 us (34%)
  matrix products  591 us (32%)
  other arithmetic  238 us (13%)
  blocking collectives  204 us (11%)
  local copies, waits for them, and re-layouts  140 us (8%)
  between operations  20.9 us (1%)
    reduce_scatter x1, waiting for transfers between devices, body(): lax.psum_scatter(ada_grad.astype(jnp.bfloat16), 'dp', scatter_dimension=0...  134 us
    reduce_scatter x1, waiting for transfers between devices, body(): lax.psum_scatter(fc1_grad.astype(jnp.bfloat16), 'dp', scatter_dimension=0...  109 us
    reduce_scatter x1, waiting for transfers between devices, body(): lax.psum_scatter(fc2_grad.astype(jnp.bfloat16), 'dp', scatter_dimension=0...  108 us
    dot_general x5, matrix products, contract_cols(): lax.dot_general(left, right, (((1,), (1,)), ((), ())), preferred_element_...  108 us
    convert_element_type x1, other arithmetic, body(): score_grad = (softmaxed * (weight_grad - row_delta)).astype(jnp.bfloat16)  103 us
    unnamed x4, blocking collectives  103 us
    dot_general x1, matrix products, body(): jnp.einsum('bqhd,bkhd->bhqk', attended_grad, value_heads, preferred_eleme...  98.5 us
    dot_general x5, matrix products, matmul(): return jnp.dot(left, right, preferred_element_type=jnp.float32)  91.4 us
  transfers between devices with their start and end apart: 19, of which 14 were waited for; matrix products, arithmetic and copies ran while one was open for 40% of the time, Pallas kernels for 0%

commit v1 on v0

--- a/solution.py
+++ b/solution.py
@@ -1,9 +1,16 @@
+import functools
+
 import jax
 import jax.numpy as jnp
 from jax import lax
+from jax.experimental import pallas as pl
+from jax.experimental.pallas import tpu as pltpu
 from jax.sharding import PartitionSpec as P
 
 HEADS = 16
+LOW = jnp.bfloat16
+WIDE = jnp.float32
+LOG2E = 1.4426950408889634
 
 
 def normalize(rows):
@@ -77,7 +84,7 @@
     )
 
 
-def body(
+def general_body(
     tokens,
     condition,
     w_ada,
@@ -366,7 +373,406 @@
     )
 
 
+NT = (((1,), (1,)), ((), ()))
+NN = (((1,), (0,)), ((), ()))
+
+
+def product(left, right, dims):
+    return lax.dot_general(left, right, dims, preferred_element_type=WIDE)
+
+
+def flat(ref):
+    value = ref[...]
+    return value.reshape(value.shape[0] * value.shape[2], value.shape[3])
+
+
+def attention_kernel(q_ref, k_ref, v_ref, o_ref, e_ref, r_ref, *, size, chunk):
+    q, k, v = flat(q_ref), flat(k_ref), flat(v_ref)
+    count = q.shape[0]
+    scaled = q.astype(WIDE) * (LOG2E * size**-0.5)
+    high = scaled.astype(LOW)
+    rest = (scaled - high.astype(WIDE)).astype(LOW)
+    v_t = v.astype(WIDE).T.astype(LOW)
+    ones = jnp.ones((16, count), LOW)
+    outs, inverses = [], []
+    for head in range(q.shape[1] // size):
+        cols = slice(head * size, (head + 1) * size)
+        keys = jnp.concatenate([k[:, cols], k[:, cols]], 1)
+        queries = jnp.concatenate([high[:, cols], rest[:, cols]], 1)
+        values = jnp.concatenate([v_t[cols], ones], 0)
+        out_parts, inverse_parts = [], []
+        for at in range(0, count, chunk):
+            scores = product(keys, queries[at : at + chunk], NT)
+            peak = jnp.max(scores, axis=0, keepdims=True)
+            weights = jnp.exp2(scores - peak).astype(LOW)
+            e_ref[0, 0, head, :, at : at + chunk] = weights
+            summed = product(values, weights, NN)
+            inverse = 1.0 / summed[size : size + 1]
+            out_parts.append(summed[:size] * inverse)
+            inverse_parts.append(inverse)
+        outs.append(jnp.concatenate(out_parts, 1))
+        inverses.append(jnp.concatenate(inverse_parts, 1))
+    o_ref[...] = jnp.concatenate(outs, 0).T.astype(LOW).reshape(o_ref.shape)
+    r_ref[0, 0] = jnp.concatenate(inverses, 0)
+
+
+def attention_back_kernel(
+    q_ref, k_ref, v_ref, o_ref, do_ref, e_ref, r_ref, dq_ref, dk_ref, dv_ref, *, size
+):
+    q, k, v = flat(q_ref), flat(k_ref), flat(v_ref)
+    do, o = flat(do_ref).astype(WIDE), flat(o_ref).astype(WIDE)
+    scale = size**-0.5
+    inverse = r_ref[0, 0]
+    prod_t = (do * o).T
+    do_t = do.T
+    k_t = (k.astype(WIDE) * scale).T.astype(LOW)
+    q_scaled = (q.astype(WIDE) * scale).astype(LOW)
+    dqs, dks, dvs = [], [], []
+    for head in range(q.shape[1] // size):
+        cols = slice(head * size, (head + 1) * size)
+        inv = inverse[head : head + 1]
+        grad_t = do_t[cols] * inv
+        delta = jnp.sum(prod_t[cols], axis=0, keepdims=True) * inv
+        weights = e_ref[0, 0, head]
+        da = product(v[:, cols], grad_t.astype(LOW), NN)
+        ds = weights * (da - delta).astype(LOW)
+        dqs.append(product(k_t[cols], ds, NN))
+        dks.append(product(ds, q_scaled[:, cols], NN))
+        dvs.append(product(weights, grad_t.T.astype(LOW), NN))
+    dq_ref[...] = jnp.concatenate(dqs, 0).T.astype(LOW).reshape(dq_ref.shape)
+    dk_ref[...] = jnp.concatenate(dks, 1).astype(LOW).reshape(dk_ref.shape)
+    dv_ref[...] = jnp.concatenate(dvs, 1).astype(LOW).reshape(dv_ref.shape)
+
+
+PARAMS = pltpu.CompilerParams(vmem_limit_bytes=56 << 20)
+
+
+def attention_blocks(half, tokens, width):
+    def columns(base):
+        return pl.BlockSpec((half, 1, tokens, width), lambda latent, pair: (0, latent, 0, base + pair))
+
+    return columns
+
+
+def attention_fore(qkv):
+    half, latents, tokens, triple = qkv.shape
+    model = triple // 3
+    size = model // HEADS
+    per = 128 // size
+    pairs = HEADS // per
+    count = half * tokens
+    columns = attention_blocks(half, tokens, 128)
+    flops = 4 * latents * HEADS * count * count * 128
+    return pl.pallas_call(
+        functools.partial(attention_kernel, size=size, chunk=count),
+        grid=(latents, pairs),
+        in_specs=[columns(0), columns(pairs), columns(2 * pairs)],
+        out_specs=[
+            columns(0),
+            pl.BlockSpec((1, 1, per, count, count), lambda latent, pair: (latent, pair, 0, 0, 0)),
+            pl.BlockSpec((1, 1, per, count), lambda latent, pair: (latent, pair, 0, 0)),
+        ],
+        out_shape=[
+            jax.ShapeDtypeStruct((half, latents, tokens, model), LOW),
+            jax.ShapeDtypeStruct((latents, pairs, per, count, count), LOW),
+            jax.ShapeDtypeStruct((latents, pairs, per, count), WIDE),
+        ],
+        compiler_params=PARAMS,
+        cost_estimate=pl.CostEstimate(
+            flops=flops, bytes_accessed=90 << 20, transcendentals=latents * HEADS * count * count
+        ),
+        name="attention_fore",
+    )(qkv, qkv, qkv)
+
+
+def attention_back(qkv, attended, attended_grad, weights, inverse):
+    half, latents, tokens, triple = qkv.shape
+    model = triple // 3
+    size = model // HEADS
+    per = 128 // size
+    pairs = HEADS // per
+    count = half * tokens
+    columns = attention_blocks(half, tokens, 128)
+    flops = 8 * latents * HEADS * count * count * 128
+    grads = jax.ShapeDtypeStruct((half, latents, tokens, model), LOW)
+    return pl.pallas_call(
+        functools.partial(attention_back_kernel, size=size),
+        grid=(latents, pairs),
+        in_specs=[
+            columns(0),
+            columns(pairs),
+            columns(2 * pairs),
+            columns(0),
+            columns(0),
+            pl.BlockSpec((1, 1, per, count, count), lambda latent, pair: (latent, pair, 0, 0, 0)),
+            pl.BlockSpec((1, 1, per, count), lambda latent, pair: (latent, pair, 0, 0)),
+        ],
+        out_specs=[columns(0)] * 3,
+        out_shape=[grads] * 3,
+        compiler_params=PARAMS,
+        cost_estimate=pl.CostEstimate(flops=flops, bytes_accessed=100 << 20, transcendentals=0),
+        name="attention_back",
+    )(qkv, qkv, qkv, attended, attended_grad, weights, inverse)
+
+
+class Wires:
+    def __init__(self, dp):
+        self.depth = dp // 4
+        index = lax.axis_index("dp")
+        self.z, self.y, self.core = index // 4, (index // 2) % 2, index % 2
+        self.x = lax.axis_index("seq")
+        self.places = [(z, y, c) for z in range(self.depth) for y in range(2) for c in range(2)]
+
+    def across(self, value):
+        return lax.ppermute(value, "seq", [(0, 1), (1, 0)])
+
+    def dp_step(self, value, move):
+        pairs = []
+        for z, y, c in self.places:
+            to_z, to_y, to_c = move(z, y, c)
+            pairs.append(((z * 2 + y) * 2 + c, (to_z * 2 + to_y) * 2 + to_c))
+        return lax.ppermute(value, "dp", pairs)
+
+    def distances(self):
+        steps, distance = [], self.depth // 2
+        while distance:
+            steps.append(distance)
+            distance //= 2
+        return steps
+
+    def bit(self, distance):
+        return (self.z // distance) % 2
+
+    def mirror(self, value, distance):
+        return self.dp_step(value, lambda z, y, c: (z ^ distance, y, c))
+
+    def beside(self, value):
+        return self.dp_step(value, lambda z, y, c: (z, 1 - y, c))
+
+    def twin(self, value):
+        return self.dp_step(value, lambda z, y, c: (z, y, 1 - c))
+
+
+def pick(value, index, axis):
+    return lax.dynamic_index_in_dim(value, index, axis, keepdims=False)
+
+
+def order_two(mine, other, index, axis, fresh=False):
+    if fresh:
+        mine, other = mine[:, None], other[:, None]
+        both = order_two(mine, other, index, 1)
+        return both.reshape((-1,) + both.shape[2:])
+    return jnp.where(
+        index == 0,
+        jnp.concatenate([mine, other], axis),
+        jnp.concatenate([other, mine], axis),
+    )
+
+
+def gather_small(wires, value):
+    held = value[None]
+    for distance in wires.distances():
+        held = order_two(held, wires.mirror(held, distance), wires.bit(distance), 0, True)
+    held = order_two(held, wires.beside(held), wires.y, 0, True)
+    held = order_two(held, wires.twin(held), wires.core, 0, True)
+    return held
+
+
+def sum_small(wires, value):
+    held = value.reshape((wires.depth, 2, 2) + value.shape[1:])
+    held = pick(held, wires.core, 2) + wires.twin(pick(held, 1 - wires.core, 2))
+    held = pick(held, wires.y, 1) + wires.beside(pick(held, 1 - wires.y, 1))
+    distances = wires.distances()
+    held = held.reshape((2,) * len(distances) + held.shape[1:])
+    for place, distance in reversed(list(enumerate(distances))):
+        bit = wires.bit(distance)
+        held = pick(held, bit, place) + wires.mirror(pick(held, 1 - bit, place), distance)
+    return held
+
+
+def gather_weight(shard):
+    return lax.all_gather(shard, "dp", axis=0, tiled=True)
+
+
+def scatter_grad(wires, grad):
+    held = lax.psum_scatter(grad, "dp", scatter_dimension=0, tiled=True)
+    halves = held.reshape(held.shape[0], 2, held.shape[1] // 2)
+    theirs = wires.across(pick(halves, 1 - wires.x, 1))
+    return pick(halves, wires.x, 1).astype(WIDE) + theirs.astype(WIDE)
+
+
+def fast_body(
+    dp,
+    tokens,
+    condition,
+    w_ada,
+    b_ada,
+    w_qkv,
+    q_bias,
+    v_bias,
+    w_proj,
+    b_proj,
+    w_fc1,
+    b_fc1,
+    w_fc2,
+    b_fc2,
+    cotangent,
+):
+    wires = Wires(dp)
+    group, tokens_here, model = tokens.shape
+    mine = group // 2
+    rows = group * tokens_here
+    x, z_y_c = wires.x, lax.axis_index("dp")
+
+    def swap(value):
+        ours = lax.dynamic_slice_in_dim(value, x * mine, mine, 0)
+        theirs = lax.dynamic_slice_in_dim(value, (1 - x) * mine, mine, 0)
+        return ours, wires.across(theirs)
+
+    def swap_back(value, kind):
+        ours, theirs = value[0].astype(kind), wires.across(value[1].astype(LOW)).astype(kind)
+        return order_two(ours, theirs, x, 0)
+
+    packed = jnp.concatenate([w_qkv, w_proj, w_fc1], axis=1)
+    theirs = wires.across(packed)
+    cuts = [w_qkv.shape[1], w_qkv.shape[1] + w_proj.shape[1]]
+    own_qkv, own_proj, own_fc1 = (
+        order_two(a, b, x, 1) for a, b in zip(jnp.split(packed, cuts, 1), jnp.split(theirs, cuts, 1))
+    )
+    own_fc2 = order_two(w_fc2, wires.across(w_fc2), x, 1)
+    full_qkv = gather_weight(own_qkv)
+    full_both = gather_weight(jnp.concatenate([own_proj, own_fc1], axis=1))
+    full_proj, full_fc1 = full_both[:, :model], full_both[:, model:]
+    full_fc2 = gather_weight(own_fc2)
+    tokens_two = jnp.stack(swap(tokens))
+    cotangent_two = jnp.stack(swap(cotangent))
+
+    vectors = (q_bias, v_bias, b_proj, b_fc1, b_fc2, b_ada)
+    sizes = [v.shape[0] for v in vectors]
+    offsets = [sum(sizes[:i]) for i in range(len(sizes))]
+    biases = jnp.concatenate(vectors)[None]
+    biases = order_two(biases, wires.across(biases), x, 0)
+    smooth, silu_pull = jax.vjp(jax.nn.silu, condition)
+    smooth_low = smooth.astype(LOW)
+    vector = jnp.concatenate([smooth_low.reshape(-1), biases.reshape(-1)])
+    vector = gather_small(wires, vector)
+    joined = vector[:, group * model :].reshape(2 * dp, -1)
+    bias_query, bias_value, bias_proj, bias_fc1, bias_fc2, bias_ada = (
+        joined[:, o : o + n].reshape(-1).astype(WIDE) for o, n in zip(offsets, sizes)
+    )
+
+    smooth_all = vector[:, : group * model].reshape(dp * group, model)
+    ada_rows = w_ada.shape[0]
+    smooth_mine = lax.dynamic_slice_in_dim(smooth_all, z_y_c * ada_rows, ada_rows, 1)
+    partial = matmul(smooth_mine, w_ada)
+    half_mods = sum_small(wires, partial.reshape(dp, group, -1))
+    ours, theirs = swap(half_mods)
+    mods = order_two(ours, theirs, x, 1) + bias_ada
+    pieces = [mods[None, :, None, i * model : (i + 1) * model] for i in range(6)]
+    shift_one, scale_one, gate_one, shift_two, scale_two, gate_two = pieces
+    four = (2, mine, tokens_here, model)
+
+    inputs = tokens_two.astype(WIDE)
+    normed_one, norm_pull_one = jax.vjp(normalize, inputs)
+    first_rows = (normed_one * (1.0 + scale_one) + shift_one).astype(LOW).reshape(rows, model)
+    bias_row = jnp.concatenate([bias_query, jnp.zeros_like(bias_query), bias_value])
+    qkv = (matmul(first_rows, full_qkv) + bias_row).astype(LOW)
+    qkv = qkv.reshape(2, mine, tokens_here, 3 * model)
+    attended, weights, inverse = attention_fore(qkv)
+    attended_rows = attended.reshape(rows, model)
+    attention = (matmul(attended_rows, full_proj) + bias_proj).reshape(four)
+    middle = inputs + gate_one * attention
+    normed_two, norm_pull_two = jax.vjp(normalize, middle)
+    second_rows = (normed_two * (1.0 + scale_two) + shift_two).astype(LOW).reshape(rows, model)
+    hidden = matmul(second_rows, full_fc1) + bias_fc1
+    active, gelu_pull = jax.vjp(gelu_tanh, hidden)
+    active_low = active.astype(LOW)
+    branch = (matmul(active_low, full_fc2) + bias_fc2).reshape(four)
+    output = swap_back((middle + gate_two * branch).astype(LOW), LOW)
+
+    grad_out = cotangent_two.astype(WIDE)
+    gate_two_grad = jnp.sum(grad_out * branch, axis=(0, 2))
+    branch_grad = (gate_two * grad_out).astype(LOW).reshape(rows, model)
+    fc2_bias_grad = jnp.sum(branch_grad.astype(WIDE), axis=0)
+    fc2_grad = scatter_grad(wires, contract_rows(active_low, branch_grad).astype(LOW))
+    active_grad = contract_cols(branch_grad, full_fc2)
+    hidden_grad = gelu_pull(active_grad)[0].astype(LOW)
+    fc1_bias_grad = jnp.sum(hidden_grad.astype(WIDE), axis=0)
+    fc1_grad = scatter_grad(wires, contract_rows(second_rows, hidden_grad).astype(LOW))
+    second_grad = contract_cols(hidden_grad, full_fc1).reshape(four)
+    shift_two_grad = jnp.sum(second_grad, axis=(0, 2))
+    scale_two_grad = jnp.sum(second_grad * normed_two, axis=(0, 2))
+    middle_grad = grad_out + norm_pull_two(second_grad * (1.0 + scale_two))[0]
+    gate_one_grad = jnp.sum(middle_grad * attention, axis=(0, 2))
+    attention_grad = (gate_one * middle_grad).astype(LOW).reshape(rows, model)
+    proj_bias_grad = jnp.sum(attention_grad.astype(WIDE), axis=0)
+    proj_grad = scatter_grad(wires, contract_rows(attended_rows, attention_grad).astype(LOW))
+    attended_grad = contract_cols(attention_grad, full_proj).astype(LOW).reshape(four)
+    dq, dk, dv = attention_back(qkv, attended, attended_grad, weights, inverse)
+    joint = jnp.concatenate([d.reshape(rows, model) for d in (dq, dk, dv)], axis=-1)
+    query_bias_grad = jnp.sum(dq.astype(WIDE), axis=(0, 1, 2))
+    value_bias_grad = jnp.sum(dv.astype(WIDE), axis=(0, 1, 2))
+    qkv_grad = scatter_grad(wires, contract_rows(first_rows, joint).astype(LOW))
+    first_grad = contract_cols(joint, full_qkv).reshape(four)
+    shift_one_grad = jnp.sum(first_grad, axis=(0, 2))
+    scale_one_grad = jnp.sum(first_grad * normed_one, axis=(0, 2))
+    input_grad = swap_back(middle_grad + norm_pull_one(first_grad * (1.0 + scale_one))[0], WIDE)
+
+    mods_grad = jnp.concatenate(
+        [shift_one_grad, scale_one_grad, gate_one_grad, shift_two_grad, scale_two_grad, gate_two_grad],
+        axis=-1,
+    ).astype(LOW)
+    halves = mods_grad.reshape(mine, 2, 3 * model)
+    group_grad = order_two(
+        pick(halves, x, 1), wires.across(pick(halves, 1 - x, 1)), x, 0
+    )
+    all_grad = gather_small(wires, group_grad).reshape(dp * group, -1)
+    ada_grad = contract_rows(smooth_mine, all_grad)
+    half_sum = jnp.sum(all_grad.astype(WIDE), axis=0)
+    both_sums = order_two(half_sum, wires.across(half_sum), x, 0)
+    ada_bias_grad = lax.dynamic_slice_in_dim(
+        both_sums, (z_y_c * 2 + x) * b_ada.shape[0], b_ada.shape[0], 0
+    )
+    smooth_part = contract_cols(all_grad, w_ada)
+    smooth_part = smooth_part + wires.across(smooth_part)
+    sums = (query_bias_grad, value_bias_grad, proj_bias_grad, fc1_bias_grad, fc2_bias_grad)
+    bias_sums = jnp.concatenate([v.reshape(2 * dp, -1) for v in sums], axis=1).reshape(dp, 2, -1)
+    bias_sums = sum_small(wires, bias_sums)
+    owned = pick(bias_sums, x, 0) + wires.across(pick(bias_sums, 1 - x, 0))
+    spread = lax.all_to_all(
+        smooth_part.reshape(dp, group, ada_rows), "dp", 0, 0, tiled=False
+    )
+    smooth_grad = jnp.swapaxes(spread, 0, 1).reshape(group, model)
+    condition_grad = silu_pull(smooth_grad)[0]
+
+    bias_grads = [owned[o : o + n] for o, n in zip(offsets, sizes[:5])]
+    return (
+        output,
+        input_grad,
+        condition_grad,
+        ada_grad,
+        ada_bias_grad,
+        qkv_grad,
+        bias_grads[0],
+        bias_grads[1],
+        proj_grad,
+        bias_grads[2],
+        fc1_grad,
+        bias_grads[3],
+        fc2_grad,
+        bias_grads[4],
+    )
+
+
 def solution(mesh):
+    sizes = dict(mesh.shape)
+
+    def body(tokens, *others):
+        split = sizes["seq"] == 2 and sizes["dp"] % 4 == 0 and tokens.shape[0] % 2 == 0
+        if split:
+            return fast_body(sizes["dp"], tokens, *others)
+        return general_body(tokens, *others)
+
     return jax.shard_map(
         body,
         mesh=mesh,

time: 1820 us -> 925 us (0.51)
  waiting for transfers between devices: 618 us -> 292 us
  matrix products: 591 us -> 267 us
  blocking collectives: 204 us -> 0 us
  Pallas kernels: 0 us -> 135 us
  other arithmetic: 238 us -> 124 us
  local copies, waits for them, and re-layouts: 140 us -> 44.5 us
  starting transfers between devices: 1.03 us -> 41.7 us
    reduce_scatter x12 -> x4, waiting for transfers between devices: 447 us -> 97.8 us  [scatter_grad(): held = lax.psum_scatter(grad, 'dp', scatter_dimension=0, tiled=True)]
    dot_general x6 -> x0, matrix products: 308 us -> none  [the longest x1 98.5 us: body(): jnp.einsum('bqhd,bkhd->bhqk', attended_grad, value_heads, preferred_eleme...]
    ppermute x0 -> x32, waiting for transfers between devices: none -> 188 us  [the longest x16 146 us: across(): return lax.ppermute(value, 'seq', [(0, 1), (1, 0)])]
    all_gather x7 -> x3, waiting for transfers between devices: 170 us -> 0.01 us  [gather_weight(): return lax.all_gather(shard, 'dp', axis=0, tiled=True)]
    pallas_call x0 -> x2, Pallas kernels: none -> 135 us  [the longest x1 74.8 us: attention_back(): pl.pallas_call(functools.partial(attention_back_kernel, size=size), grid=...]
    convert_element_type x21 -> x7, other arithmetic: 123 us -> 18.2 us  [the longest x1 5.87 us: fast_body(): (normed_one * (1.0 + scale_one) + shift_one).astype(LOW)]
    unnamed x4 -> x0, blocking collectives: 103 us -> none
    all_gather x8 -> x0, blocking collectives: 92.2 us -> none  [the longest x1 17.6 us: collect_fore(): lax.all_gather(inner[5], 'dp', axis=0, tiled=True)]
  transfers between devices with their start and end apart: 19 -> 40, of which waited for: 14 -> 20; matrix products, arithmetic and copies ran while one was open for 40% -> 30% of each run, Pallas kernels for 0% -> 7%
where the time goes in v1:
time: 925 us; the launch traced here: 920 us
  waiting for transfers between devices  292 us (32%)
  matrix products  267 us (29%)
  Pallas kernels  135 us (15%)
  other arithmetic  124 us (13%)
  local copies, waits for them, and re-layouts  44.5 us (5%)
  starting transfers between devices  41.7 us (5%)
  between operations  15.4 us (2%)
    ppermute x16, waiting for transfers between devices, across(): return lax.ppermute(value, 'seq', [(0, 1), (1, 0)])  146 us
    dot_general x5, matrix products, contract_cols(): lax.dot_general(left, right, (((1,), (1,)), ((), ())), preferred_element_...  102 us
    reduce_scatter x4, waiting for transfers between devices, scatter_grad(): held = lax.psum_scatter(grad, 'dp', scatter_dimension=0, tiled=True)  97.8 us
    dot_general x5, matrix products, matmul(): return jnp.dot(left, right, preferred_element_type=jnp.float32)  89.4 us
    dot_general x5, matrix products, contract_rows(): lax.dot_general(left, right, (((0,), (0,)), ((), ())), preferred_element_...  75.7 us
    pallas_call x1, Pallas kernels, attention_back(): pl.pallas_call(functools.partial(attention_back_kernel, size=size), grid=...  74.8 us
    pallas_call x1, Pallas kernels, attention_fore(): pl.pallas_call(functools.partial(attention_kernel, size=size, chunk=count...  60.6 us
    ppermute x16, waiting for transfers between devices, dp_step(): return lax.ppermute(value, 'dp', pairs)  42.2 us
  transfers between devices with their start and end apart: 40, of which 20 were waited for; matrix products, arithmetic and copies ran while one was open for 30% of the time, Pallas kernels for 7%

profile of v1, /device:TPU:0, one launch (start us, length us, event | category | flops | bytes accessed | tf_op | source)
XLA Modules:
  0.0 919.8 jit_solution(11047584860390810074)
XLA Ops:
  8.4 3.0 collective-permute-start.11
  11.4 11.9 %collective-permute-done.11 = bf16[64,4096]{1,0:T(8,128)(2,1)S(1)} collective-permute-done((bf16[64,4096]{1,0:T(8,128)(2,1)S(1)}, bf16[64,4096]{1,0:T(8,128)(2,1)S(1)}, u32[]{:S(2)}, u32[]{:S(2)}) %collective-permute-start.11) | collective-permute-done | bytes 524320 | tf_op jit(solution)/shard_map/ppermute | solution.py:527
  28.3 4.1 concatenate.242
  36.2 2.9 collective-permute-start.2
  43.5 3.0 collective-permute-done.3
  56.0 5.1 dynamic-slice_bitcast_fusion.1
  72.5 6.6 collective-permute-done.7
  80.3 10.5 %collective-permute-done.8 = f32[2,4,3072]{2,1,0:T(4,128)S(1)} collective-permute-done((f32[2,4,3072]{2,1,0:T(4,128)S(1)}, f32[2,4,3072]{2,1,0:T(4,128)S(1)}, u32[]{:S(2)}, u32[]{:S(2)}) %collective-permute-start.8) | collective-permute-done | bytes 98336 | tf_op jit(solution)/shard_map/ppermute | solution.py:534
  92.7 3.2 collective-permute-done.9
  96.2 58.2 %collective-permute-done.10 = f32[2,3072]{1,0:T(2,128)S(1)} collective-permute-done((f32[2,3072]{1,0:T(2,128)S(1)}, f32[2,3072]{1,0:T(2,128)S(1)}, u32[]{:S(2)}, u32[]{:S(2)}) %collective-permute-start.10) | collective-permute-done | bytes 24608 | tf_op jit(solution)/shard_map/ppermute | solution.py:527
  160.6 4.2 fusion.20
  164.9 5.9 fusion.13
  170.7 19.3 %add_convert_fusion = bf16[2048,3072]{1,0:T(8,128)(2,1)} fusion(bf16[2048,1024]{1,0:T(8,128)(2,1)} %fusion.13, bf16[1024,3072]{1,0:T(8,128)(2,1)} %all-gather.4.cloned.1.call-done, f32[3072]{0:T(1024)S(1)} %pad_maximum_fusion.8), kind=kOutput, calls=%fused_computation.11 | convolution fusion | flops 12897484800 | bytes 23080960 | tf_op jit(solution)/shard_map/dot_general | solution.py:26
  190.1 60.6 %attention_fore.1 = (bf16[2,2,512,1024]{3,2,1,0:T(8,128)(2,1)}, bf16[2,8,2,1024,1024]{4,3,2,1,0:T(8,128)(2,1)}, f32[2,8,2,1024]{3,2,1,0:T(2,128)}) custom-call(bf16[2,2,512,3072]{3,2,1,0:T(8,128)(2,1)} %bitcast.280, bf16[2,2,512,3072]{3,2,1,0:T(8,128)(2,1)} %bitcast.281, bf16[2,2,512,3072]{3,2,1,0:T(8,128)(2,1)} %bitcast.282), custom_call_target="tpu_custom_call" | custom-call | flops 17179869184 | bytes 94371840 | tf_op jit(solution)/shard_map/attention_fore/pallas_call | solution.py:466
  250.7 15.0 %fusion.74 = (f32[2048]{0:T(1024)S(1)}, f32[2048,1024]{1,0:T(8,128)}, f32[2048,1024]{1,0:T(8,128)}) fusion(f32[2,1024]{1,0:T(2,128)S(1)} %get-tuple-element.65, bf16[1,2,512,1024]{3,2,1,0:T(8,128)(2,1)} %bitcast.1, bf16[1,2,512,1024]{3,2,1,0:T(8,128)(2,1)S(1)} %get-tuple-element.50, f32[1024]{0:T(1024)S(1)} %reshape.744, bf16[2048,1024]{1,0:T(8,128)(2,1)} %bitcast.242, ...), kind=kOutput, calls=%fused_computation.221 | convolution fusion | flops 4307548160 | bytes 27283456 | tf_op jit(solution)/shard_map/dot_general | solution.py:26
  266.3 4.2 multiply_reduce_fusion.3
  272.1 3.3 fusion.17
  277.4 31.4 %multiply_convert_fusion = (bf16[2048,4096]{1,0:T(8,128)(2,1)}, f32[2048,4096]{1,0:T(8,128)}) fusion(f32[4096]{0:T(1024)S(1)} %fusion.55, bf16[2048,1024]{1,0:T(8,128)(2,1)S(1)} %fusion.17, bf16[1024,5120]{1,0:T(8,128)(2,1)S(1)} %copy-done.13), kind=kOutput, calls=%fused_computation.10 | convolution fusion | flops 17263755264 | bytes 62930944 | tf_op jit(solution)/shard_map/dot_general | solution.py:26
  308.8 47.9 %convert_reduce_fusion = (f32[4096]{0:T(1024)}, bf16[2048,4096]{1,0:T(8,128)(2,1)}) fusion(f32[2048,4096]{1,0:T(8,128)} %get-tuple-element.94, f32[4096]{0:T(1024)S(1)} %fusion.55, bf16[2048,1024]{1,0:T(8,128)(2,1)} %fusion.20, bf16[4096,1024]{1,0:T(8,128)(2,1)} %all-gather.8.cloned.1.call-done), kind=kOutput, calls=%fused_computation.9 | convolution fusion | flops 17372803072 | bytes 62947328 | tf_op jit(solution)/shard_map/dot_general | solution.py:36
  356.7 25.4 %multiply_reduce_fusion.2 = (f32[2048]{0:T(1024)S(1)}, f32[2048,1024]{1,0:T(8,128)}) fusion(f32[2048,1024]{1,0:T(8,128)} %get-tuple-element.44, f32[2,1024]{1,0:T(2,128)S(1)} %get-tuple-element.60, f32[2048]{0:T(1024)S(1)} %broadcast_multiply_fusion, bf16[2048,4096]{1,0:T(8,128)(2,1)} %get-tuple-element.96, bf16[1024,5120]{1,0:T(8,128)(2,1)} %all-gather.6.cloned.1.call-done), kind=kOutput, calls=%fused_computation.63 | convolution fusion | flops 17188255744 | bytes 41967616 | tf_op jit(solution)/shard_map/dot_general | solution.py:36
  382.2 9.8 %fusion.73 = (f32[2048]{0:T(1024)S(1)}, f32[2048,1024]{1,0:T(8,128)}) fusion(f32[2048]{0:T(1024)S(1)} %multiply_multiply_fusion.4, f32[2048,1024]{1,0:T(8,128)} %get-tuple-element.44, f32[2048]{0:T(1024)S(1)} %broadcast_multiply_fusion, f32[2048]{0:T(1024)S(1)} %get-tuple-element.77, f32[2048,1024]{1,0:T(8,128)} %get-tuple-element.90, ...), kind=kLoop, calls=%fused_computation.220 | loop fusion | flops 14678016 | bytes 25206784 | tf_op jit(solution)/shard_map/transpose(jvp())/reduce_sum | solution.py:17
  392.0 5.5 convert_reduce_fusion.3
  397.5 7.7 convolution_convert_fusion.3
  405.2 74.8 %attention_back.1 = (bf16[2,2,512,1024]{3,2,1,0:T(8,128)(2,1)}, bf16[2,2,512,1024]{3,2,1,0:T(8,128)(2,1)}, bf16[2,2,512,1024]{3,2,1,0:T(8,128)(2,1)}) custom-call(bf16[2,2,512,3072]{3,2,1,0:T(8,128)(2,1)} %bitcast.283, bf16[2,2,512,3072]{3,2,1,0:T(8,128)(2,1)} %bitcast.284, bf16[2,2,512,3072]{3,2,1,0:T(8,128)(2,1)} %bitcast.285, ...), custom_call_target="tpu_custom_call" | custom-call | flops 34359738368 | bytes 104857600 | tf_op jit(solution)/shard_map/attention_back/pallas_call | solution.py:498
  480.0 20.7 %fusion.27 = (f32[2048]{0:T(1024)S(1)}, f32[2048,1024]{1,0:T(8,128)}) fusion(f32[2,1024]{1,0:T(2,128)S(1)} %copy-done.20, f32[2048]{0:T(1024)S(1)} %bitcast.267, bf16[1,2,512,1024]{3,2,1,0:T(8,128)(2,1)} %bitcast.1, bf16[1,2,512,1024]{3,2,1,0:T(8,128)(2,1)S(1)} %copy-done.3, bf16[1024,3072]{1,0:T(8,128)(2,1)} %all-gather.4.cloned.1.call-done, ...), kind=kOutput, calls=%fused_computation.52 | convolution fusion | flops 12935231488 | bytes 31481856 | tf_op jit(solution)/shard_map/dot_general | solution.py:36
  500.8 5.9 fusion.11
  506.9 16.2 %fusion.10 = (f32[2,2,512,1024]{3,2,1,0:T(8,128)}, f32[2,2,512,1024]{3,2,1,0:T(8,128)S(1)}) fusion(f32[2,2,512]{2,1,0:T(2,128)S(1)} %div.114, f32[2,2,512]{2,1,0:T(2,128)S(1)} %get-tuple-element.79, f32[2,2,512]{2,1,0:T(2,128)S(1)} %get-tuple-element.78, f32[2,1024]{1,0:T(2,128)S(1)} %copy-done.20, f32[2,2,512]{2,1,0:T(2,128)S(1)} %copy-done.18, ...), kind=kLoop, calls=%fused_computation.26 | loop fusion | flops 46137344 | bytes 50421760 | tf_op jit(solution)/shard_map/add | solution.py:719
  523.1 3.3 copy-done.7
  526.4 5.8 bitcast_convert_fusion
  532.2 20.2 %convolution_convert_fusion.2 = bf16[1024,3072]{1,0:T(8,128)(2,1)} fusion(bf16[2048,1024]{1,0:T(8,128)(2,1)} %fusion.13, bf16[2048,1024]{1,0:T(8,128)(2,1)} %bitcast.246, bf16[2048,1024]{1,0:T(8,128)(2,1)} %bitcast.287, bf16[2048,1024]{1,0:T(8,128)(2,1)} %bitcast.244), kind=kOutput, calls=%fused_computation.72 | convolution fusion | flops 12925796352 | bytes 23068672 | tf_op jit(solution)/shard_map/dot_general | solution.py:30
  552.5 24.1 %convolution_convert_fusion = bf16[4096,1024]{1,0:T(8,128)(2,1)} fusion(bf16[2048,4096]{1,0:T(8,128)(2,1)} %get-tuple-element.93, bf16[2048,1024]{1,0:T(8,128)(2,1)} %fusion.20), kind=kOutput, calls=%fused_computation.66 | convolution fusion | flops 17184063488 | bytes 29360128 | tf_op jit(solution)/shard_map/dot_general | solution.py:30
  577.4 23.7 %convolution_convert_fusion.1 = bf16[1024,4096]{1,0:T(8,128)(2,1)} fusion(bf16[2048,1024]{1,0:T(8,128)(2,1)} %copy-done.9, bf16[2048,4096]{1,0:T(8,128)(2,1)} %get-tuple-element.96), kind=kOutput, calls=%fused_computation.67 | convolution fusion | flops 17184063488 | bytes 29360128 | tf_op jit(solution)/shard_map/dot_general | solution.py:30
  601.1 23.3 %convolution_add_fusion = f32[2048,1024]{1,0:T(8,128)S(1)} fusion(bf16[2048,4096]{1,0:T(8,128)(2,1)} %get-tuple-element.93, bf16[4096,1024]{1,0:T(8,128)(2,1)} %all-gather.8.cloned.1.call-done, f32[1024]{0:T(1024)S(1)} %reshape.746), kind=kOutput, calls=%fused_computation.74 | convolution fusion | flops 17181966336 | bytes 33558528 | tf_op jit(solution)/shard_map/dot_general | solution.py:26
  624.5 4.3 convert_reduce_fusion.2
  628.9 5.2 convert_reduce_fusion.4
  634.7 18.7 %multiply_reduce_fusion = (bf16[2,1024]{1,0:T(2,128)(2,1)S(1)}, bf16[2,1024]{1,0:T(2,128)(2,1)S(1)}, bf16[2,1024]{1,0:T(2,128)(2,1)S(1)}, bf16[2,1024]{1,0:T(2,1...) fusion(f32[2,2,512,1024]{3,2,1,0:T(8,128)} %bitcast.237, ...), kind=kLoop, calls=%fused_computation.61 | loop fusion | flops 48224256 | bytes 58789888 | tf_op jit(solution)/shard_map/reduce_sum | solution.py:704
  656.6 3.9 fusion.38
  665.2 3.5 collective-permute-start.27
  671.4 3.7 collective-permute-done.17
  675.2 6.7 collective-permute-done.18
  684.8 68.4 %collective-permute-done.28 = f32[256]{0:T(256)S(1)} collective-permute-done((f32[256]{0:T(256)S(1)}, f32[256]{0:T(256)S(1)}, u32[]{:S(2)}, u32[]{:S(2)}) %collective-permute-start.28) | collective-permute-done | bytes 1056 | tf_op jit(solution)/shard_map/ppermute | solution.py:527
  762.1 5.0 all-to-all-start
  767.8 5.8 all-to-all-done
  775.6 4.0 convert_element_type.228
  779.7 3.9 maximum_select_fusion.1
  786.1 9.4 %maximum_select_fusion = f32[4,512,1024]{2,1,0:T(8,128)} fusion(f32[2,512,1024]{2,1,0:T(8,128)} %convert_element_type.228, f32[2,512,1024]{2,1,0:T(8,128)} %slice_bitcast_fusion, pred[]{:T(512)S(6)} %eq.39), kind=kLoop, calls=%fused_computation.34 | loop fusion | flops 6291456 | bytes 16777216 | tf_op jit(solution)/shard_map/jit(_where)/select_n | solution.py:565
  803.1 97.8 %reduce-scatter.9.cloned.1.call-done = bf16[64,4096]{1,0:T(8,128)(2,1)} async-done(((bf16[1024,4096]{1,0:T(8,128)(2,1)}), bf16[64,4096]{1,0:T(8,128)(2,1)}) %reduce-scatter.9.cloned.1.call-update) | async-done | bytes 524304 | tf_op jit(solution)/shard_map/reduce_scatter | solution.py:598
  906.8 5.0 collective-permute-done.30
  (288 shorter events, 92.2 us)
Async XLA Ops:
  7.2 163.5 %all-gather.4.cloned.1.call-start = ((), (), s32[]{:S(2)}) async-start(), calls=%async_computation.5 | async-start | bytes 6684672 | tf_op jit(solution)/shard_map/all_gather | solution.py:594
  8.4 14.9 %collective-permute-start.11 = (bf16[64,4096]{1,0:T(8,128)(2,1)S(1)}, bf16[64,4096]{1,0:T(8,128)(2,1)S(1)}, u32[]{:S(2)}, u32[]{:S(2)}) collective-permute-start(bf16[64,4096]{1,0:T(8,128)(2,1)S(1)} %pad_maximum_fusion.7), channel_id=1, source_target_pairs={{0,1},{1,0},{2,3},{3,2},{4,5},{5,4},{6,7},{7,6},{8,9},{9,8},{10,11... | collective-permute-start | bytes 1572872 | tf_op jit(solution)/shard_map/ppermute | solution.py:527
  25.2 225.5 %all-gather.6.cloned.1.call-start = ((), (), s32[]{:S(2)}) async-start(), calls=%async_computation.6 | async-start | bytes 11141120 | tf_op jit(solution)/shard_map/all_gather | solution.py:594
  28.3 280.5 %all-gather.8.cloned.1.call-start = ((), (), s32[]{:S(2)}) async-start(), calls=%async_computation.7 | async-start | bytes 8912896 | tf_op jit(solution)/shard_map/all_gather | solution.py:594
  32.5 3.6 collective-permute-start.1
  36.2 5.7 collective-permute-start.2
  42.0 4.4 collective-permute-start.3
  46.6 4.1 collective-permute-start.4
  50.9 1.3 collective-permute-start.5
  53.9 11.8 %collective-permute-start.6 = (f32[4,2,4,3072]{3,2,1,0:T(4,128)}, f32[4,2,4,3072]{3,2,1,0:T(4,128)}, u32[]{:S(2)}, u32[]{:S(2)}) collective-permute-start(f32[4,2,4,3072]{3,2,1,0:T(4,128)} %dynamic-slice_bitcast_fusion.2), channel_id=1, source_target_pairs={{0,2},{2,0},{4,6},{6,4},{8,10},{10,8},{12,14},{14,12},{16,18},{18,... | collective-permute-start | bytes 1179656 | tf_op jit(solution)/shard_map/ppermute | solution.py:534
  54.1 16.0 %collective-permute-start.12 = (bf16[256,512]{1,0:T(8,128)(2,1)}, bf16[256,512]{1,0:T(8,128)(2,1)}, u32[]{:S(2)}, u32[]{:S(2)}) collective-permute-start(bf16[256,512]{1,0:T(8,128)(2,1)} %param.25), channel_id=1, source_target_pairs={{0,1},{1,0},{2,3},{3,2},{4,5},{5,4},{6,7},{7,6},{8,9},{9,8},{10,11... | collective-permute-start | bytes 786440 | tf_op jit(solution)/shard_map/ppermute | solution.py:527
  61.1 189.6 %copy-start.2 = (bf16[1,2,512,1024]{3,2,1,0:T(8,128)(2,1)}, bf16[1,2,512,1024]{3,2,1,0:T(8,128)(2,1)S(1)}, u32[]{:S(2)}) copy-start(bf16[1,2,512,1024]{3,2,1,0:T(8,128)(2,1)S(1)} %get-tuple-element.50) | copy-start | bytes 6291460
  61.1 93.4 %collective-permute-start = (bf16[2,512,1024]{2,1,0:T(8,128)(2,1)}, bf16[2,512,1024]{2,1,0:T(8,128)(2,1)}, u32[]{:S(2)}, u32[]{:S(2)}) collective-permute-start(bf16[2,512,1024]{2,1,0:T(8,128)(2,1)} %get-tuple-element.51), channel_id=1, source_target_pairs={{0,1},{1,0},{2,3},{3,2},{4,5},{5,4},{6,7},{7,6},{8,9},{9,8},{10,11... | collective-permute-start | bytes 6291464 | tf_op jit(solution)/shard_map/ppermute | solution.py:527
  63.8 96.8 %collective-permute-start.14 = (bf16[2,512,1024]{2,1,0:T(8,128)(2,1)}, bf16[2,512,1024]{2,1,0:T(8,128)(2,1)}, u32[]{:S(2)}, u32[]{:S(2)}) collective-permute-start(bf16[2,512,1024]{2,1,0:T(8,128)(2,1)} %get-tuple-element.47), channel_id=1, source_target_pairs={{0,1},{1,0},{2,3},{3,2},{4,5},{5,4},{6,7},{7,6},{8,9},{9,8},{10,11... | collective-permute-start | bytes 6291464 | tf_op jit(solution)/shard_map/ppermute | solution.py:527
  67.6 11.5 %collective-permute-start.7 = (f32[4,4,3072]{2,1,0:T(4,128)S(1)}, f32[4,4,3072]{2,1,0:T(4,128)S(1)}, u32[]{:S(2)}, u32[]{:S(2)}) collective-permute-start(f32[4,4,3072]{2,1,0:T(4,128)S(1)} %dynamic-slice_bitcast_fusion.3), channel_id=1, source_target_pairs={{0,4},{2,6},{4,0},{6,2},{8,12},{10,14},{12,8},{14,10},{16,20},{18,... | collective-permute-start | bytes 589832 | tf_op jit(solution)/shard_map/ppermute | solution.py:534
  72.3 711.3 %reduce-scatter.7.cloned.1.call-start = ((), (), s32[]{:S(2)}) async-start(), calls=%async_computation.9 | async-start | bytes 2228224 | tf_op jit(solution)/shard_map/reduce_scatter | solution.py:598
  80.2 10.6 %collective-permute-start.8 = (f32[2,4,3072]{2,1,0:T(4,128)S(1)}, f32[2,4,3072]{2,1,0:T(4,128)S(1)}, u32[]{:S(2)}, u32[]{:S(2)}) collective-permute-start(f32[2,4,3072]{2,1,0:T(4,128)S(1)} %dynamic-slice_bitcast_fusion.4), channel_id=1, source_target_pairs={{0,8},{2,10},{4,12},{6,14},{8,0},{10,2},{12,4},{14,6},{16,24},{18,... | collective-permute-start | bytes 294920 | tf_op jit(solution)/shard_map/ppermute | solution.py:534
  90.9 5.1 collective-permute-start.9
  96.0 58.5 %collective-permute-start.10 = (f32[2,3072]{1,0:T(2,128)S(1)}, f32[2,3072]{1,0:T(2,128)S(1)}, u32[]{:S(2)}, u32[]{:S(2)}) collective-permute-start(f32[2,3072]{1,0:T(2,128)S(1)} %get-tuple-element.67), channel_id=1, source_target_pairs={{0,1},{1,0},{2,3},{3,2},{4,5},{5,4},{6,7},{7,6},{8,9},{9,8},{10,11... | collective-permute-start | bytes 73736 | tf_op jit(solution)/shard_map/ppermute | solution.py:527
  96.2 64.4 %copy-start.4 = (bf16[1,2,512,1024]{3,2,1,0:T(8,128)(2,1)S(1)}, bf16[1,2,512,1024]{3,2,1,0:T(8,128)(2,1)}, u32[]{:S(2)}) copy-start(bf16[1,2,512,1024]{3,2,1,0:T(8,128)(2,1)} %get-tuple-element.46) | copy-start | bytes 6291460
  405.2 74.8 %copy-start.3 = (bf16[1,2,512,1024]{3,2,1,0:T(8,128)(2,1)S(1)}, bf16[1,2,512,1024]{3,2,1,0:T(8,128)(2,1)}, u32[]{:S(2)}) copy-start(bf16[1,2,512,1024]{3,2,1,0:T(8,128)(2,1)} %copy-done.2) | copy-start | bytes 6291460
  405.2 74.8 %copy-start.20 = (f32[2,1024]{1,0:T(2,128)S(1)}, f32[2,1024]{1,0:T(2,128)}, u32[]{:S(2)}) copy-start(f32[2,1024]{1,0:T(2,128)} %copy-done.19) | copy-start | bytes 24580
  405.2 74.8 %copy-start.27 = (f32[2,4,2,128]{3,1,2,0:T(4,128)S(1)}, f32[2,4,2,128]{3,1,2,0:T(4,128)}, u32[]{:S(2)}) copy-start(f32[2,4,2,128]{3,1,2,0:T(4,128)} %copy-done.26) | copy-start | bytes 24580
  532.2 264.0 %reduce-scatter.5.cloned.1.call-start = ((), (), s32[]{:S(2)}) async-start(), calls=%async_computation.8 | async-start | bytes 6684672 | tf_op jit(solution)/shard_map/reduce_scatter | solution.py:598
  552.5 246.9 %reduce-scatter.11.cloned.1.call-start = ((), (), s32[]{:S(2)}) async-start(), calls=%async_computation.11 | async-start | bytes 8912896 | tf_op jit(solution)/shard_map/reduce_scatter | solution.py:598
  576.7 324.3 %reduce-scatter.9.cloned.1.call-start = ((), (), s32[]{:S(2)}) async-start(), calls=%async_computation.10 | async-start | bytes 8912896 | tf_op jit(solution)/shard_map/reduce_scatter | solution.py:598
  634.6 20.3 %collective-permute-start.24 = (f32[4,2,2,256]{3,2,1,0:T(2,128)S(1)}, f32[4,2,2,256]{3,2,1,0:T(2,128)S(1)}, u32[]{:S(2)}, u32[]{:S(2)}) collective-permute-start(f32[4,2,2,256]{3,2,1,0:T(2,128)S(1)} %dynamic-slice_bitcast_fusion.6), channel_id=1, source_target_pairs={{0,2},{2,0},{4,6},{6,4},{8,10},{10,8},{12,14},{14,12},{16,18},{18,... | collective-permute-start | bytes 49160 | tf_op jit(solution)/shard_map/ppermute | solution.py:534
  634.7 47.6 %slice-start = ((s8[8388608]{0:T(1024)(128)(4,1)}), s8[4194304]{0:T(1024)(128)(4,1)S(1)}, s32[]{:S(2)}) async-start(s8[8388608]{0:T(1024)(128)(4,1)} %bitcast.240), calls=%async_computation.12 | async-start | bytes 8388608
  634.7 47.6 %slice-start.1 = ((s8[8388608]{0:T(1024)(128)(4,1)}), s8[4194304]{0:T(1024)(128)(4,1)S(1)}, s32[]{:S(2)}) async-start(s8[8388608]{0:T(1024)(128)(4,1)} %bitcast.240), calls=%async_computation.13 | async-start | bytes 8388608
  653.5 15.1 %collective-permute-start.16 = (bf16[2,3072]{1,0:T(2,128)(2,1)S(1)}, bf16[2,3072]{1,0:T(2,128)(2,1)S(1)}, u32[]{:S(2)}, u32[]{:S(2)}) collective-permute-start(bf16[2,3072]{1,0:T(2,128)(2,1)S(1)} %get-tuple-element.73), channel_id=1, source_target_pairs={{0,1},{1,0},{2,3},{3,2},{4,5},{5,4},{6,7},{7,6},{8,9},{9,8},{10,11... | collective-permute-start | bytes 36872 | tf_op jit(solution)/shard_map/ppermute | solution.py:527
  654.9 6.6 collective-permute-start.25
  660.5 115.2 %collective-permute-start.15 = (bf16[2,512,1024]{2,1,0:T(8,128)(2,1)}, bf16[2,512,1024]{2,1,0:T(8,128)(2,1)}, u32[]{:S(2)}, u32[]{:S(2)}) collective-permute-start(bf16[2,512,1024]{2,1,0:T(8,128)(2,1)} %fusion.38), channel_id=1, source_target_pairs={{0,1},{1,0},{2,3},{3,2},{4,5},{5,4},{6,7},{7,6},{8,9},{9,8},{10,11... | collective-permute-start | bytes 6291464 | tf_op jit(solution)/shard_map/ppermute | solution.py:527
  661.5 3.7 collective-permute-start.26
  663.4 111.7 %copy-start.30 = (f32[4,1024]{1,0:T(4,128)S(1)}, f32[4,1024]{1,0:T(4,128)}, u32[]{:S(2)}) copy-start(f32[4,1024]{1,0:T(4,128)} %param.15) | copy-start | bytes 49156
  663.4 116.3 %collective-permute-start.13 = (bf16[2,512,1024]{2,1,0:T(8,128)(2,1)}, bf16[2,512,1024]{2,1,0:T(8,128)(2,1)}, u32[]{:S(2)}, u32[]{:S(2)}) collective-permute-start(bf16[2,512,1024]{2,1,0:T(8,128)(2,1)} %get-tuple-element.49), channel_id=1, source_target_pairs={{0,1},{1,0},{2,3},{3,2},{4,5},{5,4},{6,7},{7,6},{8,9},{9,8},{10,11... | collective-permute-start | bytes 6291464 | tf_op jit(solution)/shard_map/ppermute | solution.py:527
  665.2 5.1 collective-permute-start.27
  668.7 6.4 collective-permute-start.17
  670.3 82.8 %collective-permute-start.28 = (f32[256]{0:T(256)S(1)}, f32[256]{0:T(256)S(1)}, u32[]{:S(2)}, u32[]{:S(2)}) collective-permute-start(f32[256]{0:T(256)S(1)} %bitcast.279), channel_id=1, source_target_pairs={{0,1},{1,0},{2,3},{3,2},{4,5},{5,4},{6,7},{7,6},{8,9},{9,8},{10,11... | collective-permute-start | bytes 3080 | tf_op jit(solution)/shard_map/ppermute | solution.py:527
  675.1 6.8 collective-permute-start.18
  682.0 71.7 %collective-permute-start.19 = (bf16[4,4,3072]{2,1,0:T(4,128)(2,1)S(1)}, bf16[4,4,3072]{2,1,0:T(4,128)(2,1)S(1)}, u32[]{:S(2)}, u32[]{:S(2)}) collective-permute-start(bf16[4,4,3072]{2,1,0:T(4,128)(2,1)S(1)} %bitcast.251), channel_id=1, source_target_pairs={{0,4},{2,6},{4,0},{6,2},{8,12},{10,14},{12,8},{14,10},{16,20},{18,... | collective-permute-start | bytes 294920 | tf_op jit(solution)/shard_map/ppermute | solution.py:534
  754.1 1.5 collective-permute-start.20
  756.1 11.0 %collective-permute-start.22 = (f32[3072]{0:T(1024)S(1)}, f32[3072]{0:T(1024)S(1)}, u32[]{:S(2)}, u32[]{:S(2)}) collective-permute-start(f32[3072]{0:T(1024)S(1)} %get-tuple-element.37), channel_id=1, source_target_pairs={{0,1},{1,0},{2,3},{3,2},{4,5},{5,4},{6,7},{7,6},{8,9},{9,8},{10,11... | collective-permute-start | bytes 36872 | tf_op jit(solution)/shard_map/ppermute | solution.py:527
  757.5 4.0 collective-permute-start.21
  762.1 11.5 %all-to-all-start = ((f32[16,1,256]{2,1,0:T(1,128)}), f32[16,1,256]{2,1,0:T(1,128)S(1)}, u32[]{:S(2)}, u32[]{:S(2)}) async-start(f32[16,1,256]{2,1,0:T(1,128)} %reshape.753), calls=%async_computation | async-start | bytes 32768 | tf_op jit(solution)/shard_map/all_to_all | solution.py:742
  784.9 10.7 %collective-permute-start.29 = (bf16[64,512]{1,0:T(8,128)(2,1)S(1)}, bf16[64,512]{1,0:T(8,128)(2,1)S(1)}, u32[]{:S(2)}, u32[]{:S(2)}) collective-permute-start(bf16[64,512]{1,0:T(8,128)(2,1)S(1)} %bitcast.269), channel_id=1, source_target_pairs={{0,1},{1,0},{2,3},{3,2},{4,5},{5,4},{6,7},{7,6},{8,9},{9,8},{10,11... | collective-permute-start | bytes 196616 | tf_op jit(solution)/shard_map/ppermute | solution.py:527
  798.4 106.8 %collective-permute-start.23 = (bf16[64,1536]{1,0:T(8,128)(2,1)S(1)}, bf16[64,1536]{1,0:T(8,128)(2,1)S(1)}, u32[]{:S(2)}, u32[]{:S(2)}) collective-permute-start(bf16[64,1536]{1,0:T(8,128)(2,1)S(1)} %bitcast.256), channel_id=1, source_target_pairs={{0,1},{1,0},{2,3},{3,2},{4,5},{5,4},{6,7},{7,6},{8,9},{9,8},{10,11... | collective-permute-start | bytes 589832 | tf_op jit(solution)/shard_map/ppermute | solution.py:527
  802.0 104.0 %collective-permute-start.31 = (bf16[256,512]{1,0:T(8,128)(2,1)S(1)}, bf16[256,512]{1,0:T(8,128)(2,1)S(1)}, u32[]{:S(2)}, u32[]{:S(2)}) collective-permute-start(bf16[256,512]{1,0:T(8,128)(2,1)S(1)} %bitcast.253), channel_id=1, source_target_pairs={{0,1},{1,0},{2,3},{3,2},{4,5},{5,4},{6,7},{7,6},{8,9},{9,8},{10,11... | collective-permute-start | bytes 786440 | tf_op jit(solution)/shard_map/ppermute | solution.py:527
  903.6 8.1 collective-permute-start.30
  (29 other events, 299.1 us)
Sparse Core Ops, SparseCore 0:
  25.3 69.1 all-gather.3
  97.4 87.6 all-gather.5
  187.8 73.0 all-gather.7
  532.3 62.5 reduce-scatter.6
  599.2 85.6 reduce-scatter.4
  688.9 103.5 reduce-scatter.10
  796.5 104.4 reduce-scatter.8
